TPU v7x, 256 devices: a whole 4x4x8 slice. The times are simulated.
256 devices in a mesh: dp: 2 (over x_lo), ctx: 16 (over z, x_hi), tp: 8 (over y, core).
Axes of the slice: x: 4 (x_hi: 2, x_lo: 2; x = x_hi * 2 + x_lo), y: 4, z: 8, core: 2. Of those that a mesh axis runs over, the one named last changes fastest.
Arguments:
- queries: bfloat16 [2, 8192, 8192], P('dp', ('ctx', 'tp')), may hold values from -300 to 300
- key_rows: bfloat16 [2, 8192, 1024], P('dp', ('ctx', 'tp')), may hold values from -12 to 12
- values_in: bfloat16 [2, 8192, 1024], P('dp', ('ctx', 'tp')), may hold values from -6 to 6
- out_grad: bfloat16 [2, 8192, 8192], P('dp', ('ctx', 'tp')), may hold values from -6 to 6
- send_rows: int32 [2, 128, 64], P('dp', ('ctx', 'tp')), may hold values from 0 to 63, each once within a row
- doc_lengths: int32 [2, 32], P('dp'), may hold values from 1 to 1024, 8192 in all within a row
Outputs:
- attended: bfloat16 [2, 8192, 8192], P('dp', 'ctx', 'tp')
- query_grad: bfloat16 [2, 8192, 8192], P('dp', 'ctx', 'tp')
- key_grad: bfloat16 [2, 8192, 1024], P('dp', 'ctx', 'tp')
- value_grad: bfloat16 [2, 8192, 1024], P('dp', 'ctx', 'tp')
Inputs may be any that keep to these rules, and one draw needn't show every extreme that they name: Each row send_rows[d, b] is a permutation of the 64 rows that old replica d holds in slot b; its entries e * 32 to (e + 1) * 32 - 1 name the rows that move to replica e. `doc_lengths`: each row sums to 8192; its longest document has exactly 1024 positions.
All inputs are finite; a program needn't handle non-finite values.
Results may differ from a plain program's by a relative error of at most 0.015.
Values may be sent and summed in bfloat16 or wider, within the bound.
No kernel may reach another device: no remote copies, remote signals or barrier semaphores. Data moves between devices by JAX's collectives and lax.ppermute only.
A program may use at most 64 MiB of HBM per device.

v0:
```python
import math

import jax
import jax.numpy as jnp
from jax import lax
from jax.sharding import PartitionSpec as P

HD = 128
SPAN = 2
GROUP = 8


def shifted(block, axis, distance):
    devices = range(lax.axis_size(axis))
    route = [(i - distance, i) for i in devices if i - distance in devices]
    return lax.ppermute(block, axis, route)


def segment_ids(starts, positions):
    return jnp.sum((starts[None, :] <= positions[:, None]).astype(jnp.int32), axis=1) - 1


def arrange(array, order, groups):
    picked = jnp.take(array[0], order, axis=0)
    return picked.reshape(1, groups, picked.shape[0] // groups, picked.shape[1])


def flatten(moved):
    return moved.reshape(moved.shape[0] * moved.shape[1] * moved.shape[2], moved.shape[3])


def on_device(queries, key_rows, values_in, out_grad, send_rows, doc_lengths):
    replicas = lax.axis_size("dp")
    order = send_rows[0, 0]
    query_sent = arrange(queries, order, replicas)
    key_sent = arrange(key_rows, order, replicas)
    value_sent = arrange(values_in, order, replicas)
    grad_sent = arrange(out_grad, order, replicas)
    query_moved, key_moved, value_moved, grad_moved = (
        lax.all_to_all(
            lax.all_to_all(query_sent, "dp", split_axis=1, concat_axis=1, tiled=True),
            "tp",
            split_axis=3,
            concat_axis=0,
            tiled=True,
        ),
        lax.all_to_all(
            lax.all_to_all(key_sent, "dp", split_axis=1, concat_axis=1, tiled=True),
            "tp",
            split_axis=3,
            concat_axis=0,
            tiled=True,
        ),
        lax.all_to_all(
            lax.all_to_all(value_sent, "dp", split_axis=1, concat_axis=1, tiled=True),
            "tp",
            split_axis=3,
            concat_axis=0,
            tiled=True,
        ),
        lax.all_to_all(
            lax.all_to_all(grad_sent, "dp", split_axis=1, concat_axis=1, tiled=True),
            "tp",
            split_axis=3,
            concat_axis=0,
            tiled=True,
        ),
    )
    local_query = flatten(query_moved)
    local_key = flatten(key_moved)
    local_value = flatten(value_moved)
    local_grad = flatten(grad_moved)
    block_rows = local_query.shape[0]
    width = (SPAN + 1) * block_rows
    lengths = doc_lengths[0]
    starts = jnp.cumsum(lengths) - lengths
    first = lax.axis_index("ctx") * block_rows
    query_pos = first + jnp.arange(block_rows, dtype=jnp.int32)
    key_pos = first - SPAN * block_rows + jnp.arange(width, dtype=jnp.int32)
    allowed = (key_pos[None, :] <= query_pos[:, None]) & (
        segment_ids(starts, key_pos)[None, :] == segment_ids(starts, query_pos)[:, None]
    )
    fetched = []
    for offset in range(SPAN, 0, -1):
        fetched.append(shifted((local_key, local_value), "ctx", offset))
    window_key = jnp.concatenate([piece[0] for piece in fetched] + [local_key], axis=0)
    window_value = jnp.concatenate([piece[1] for piece in fetched] + [local_value], axis=0)
    heads = local_query.shape[1] // HD
    kv_local = local_key.shape[1] // HD
    query_three = local_query.reshape(block_rows, heads, HD)
    grad_three = local_grad.reshape(block_rows, heads, HD)
    key_three = window_key.reshape(width, kv_local, HD)
    value_three = window_value.reshape(width, kv_local, HD)
    scale = 1.0 / math.sqrt(HD)

    def head_step(head, carry):
        dkey_acc, dvalue_acc, output_all, dquery_all = carry
        kv_head = head // GROUP
        query_head = lax.dynamic_index_in_dim(query_three, head, 1, keepdims=False)
        grad_head = lax.dynamic_index_in_dim(grad_three, head, 1, keepdims=False)
        key_head = lax.dynamic_index_in_dim(key_three, kv_head, 1, keepdims=False)
        value_head = lax.dynamic_index_in_dim(value_three, kv_head, 1, keepdims=False)
        scores = (
            jnp.einsum("qd,kd->qk", query_head, key_head, preferred_element_type=jnp.float32)
            * scale
        )
        scores = jnp.where(allowed, scores, -1e30)
        top = jnp.max(scores, axis=1, keepdims=True)
        expo = jnp.exp(scores - top)
        prob = (expo / jnp.sum(expo, axis=1, keepdims=True)).astype(jnp.bfloat16)
        output = jnp.dot(prob, value_head, preferred_element_type=jnp.float32).astype(jnp.bfloat16)
        delta = jnp.sum(
            grad_head.astype(jnp.float32) * output.astype(jnp.float32), axis=1, keepdims=True
        )
        dprob = jnp.einsum("qd,kd->qk", grad_head, value_head, preferred_element_type=jnp.float32)
        dscore = (prob.astype(jnp.float32) * (dprob - delta) * scale).astype(jnp.bfloat16)
        dquery = jnp.dot(dscore, key_head, preferred_element_type=jnp.float32).astype(jnp.bfloat16)
        dkey = jnp.einsum("qk,qd->kd", dscore, query_head, preferred_element_type=jnp.float32)
        dvalue = jnp.einsum("qk,qd->kd", prob, grad_head, preferred_element_type=jnp.float32)
        dkey_acc = lax.dynamic_update_index_in_dim(
            dkey_acc,
            lax.dynamic_index_in_dim(dkey_acc, kv_head, 1, keepdims=False) + dkey,
            kv_head,
            1,
        )
        dvalue_acc = lax.dynamic_update_index_in_dim(
            dvalue_acc,
            lax.dynamic_index_in_dim(dvalue_acc, kv_head, 1, keepdims=False) + dvalue,
            kv_head,
            1,
        )
        output_all = lax.dynamic_update_index_in_dim(output_all, output, head, 1)
        dquery_all = lax.dynamic_update_index_in_dim(dquery_all, dquery, head, 1)
        return (dkey_acc, dvalue_acc, output_all, dquery_all)

    start_carry = (
        jnp.zeros((width, kv_local, HD), jnp.float32),
        jnp.zeros((width, kv_local, HD), jnp.float32),
        jnp.zeros((block_rows, heads, HD), jnp.bfloat16),
        jnp.zeros((block_rows, heads, HD), jnp.bfloat16),
    )
    dkey_acc, dvalue_acc, output_all, dquery_all = lax.fori_loop(0, heads, head_step, start_carry)
    parts_key = dkey_acc.reshape(width, kv_local * HD)
    parts_value = dvalue_acc.reshape(width, kv_local * HD)
    own_begin = SPAN * block_rows
    own_key = parts_key[own_begin:]
    own_value = parts_value[own_begin:]
    for offset in range(1, SPAN + 1):
        begin = (SPAN - offset) * block_rows
        returned = shifted(
            (parts_key[begin : begin + block_rows], parts_value[begin : begin + block_rows]),
            "ctx",
            -offset,
        )
        own_key = own_key + returned[0]
        own_value = own_value + returned[1]
    attended = output_all.reshape(1, block_rows, heads * HD)
    query_grad = dquery_all.reshape(1, block_rows, heads * HD)
    key_grad = own_key.astype(jnp.bfloat16)[None]
    value_grad = own_value.astype(jnp.bfloat16)[None]
    return (attended, query_grad, key_grad, value_grad)


def solution(mesh):
    return jax.shard_map(
        on_device,
        mesh=mesh,
        in_specs=(
            P("dp", ("ctx", "tp"), None),
            P("dp", ("ctx", "tp"), None),
            P("dp", ("ctx", "tp"), None),
            P("dp", ("ctx", "tp"), None),
            P("dp", ("ctx", "tp"), None),
            P("dp", None),
        ),
        out_specs=(
            P("dp", "ctx", "tp"),
            P("dp", "ctx", "tp"),
            P("dp", "ctx", "tp"),
            P("dp", "ctx", "tp"),
        ),
        check_vma=False,
    )
```

profile of v0, /device:TPU:42, one launch (start us, length us, event | category | flops | bytes accessed | tf_op | source)
XLA Modules:
  0.0 286.9 jit_solution(2714608951222426988)
XLA Ops:
  6.3 5.5 %all_to_all.80 = bf16[1,2,32,1024]{3,2,0,1:T(8,128)(2,1)S(1)} all-to-all(bf16[1,2,32,1024]{3,2,0,1:T(8,128)(2,1)S(1)} %bitcast.188), channel_id=1, replica_groups=mesh['dp'=2,'ctx'=16,'tp'=8] {'dp'}, dimensions={1} | all-to-all | bytes 262144 | tf_op jit(solution)/shard_map/all_to_all | solution.py:48
  11.8 5.4 %all-to-all-start.6 = ((bf16[1,2,32,1024]{3,2,0,1:T(8,128)(2,1)}), bf16[1,2,32,1024]{3,2,0,1:T(8,128)(2,1)S(1)}, u32[]{:S(2)}, u32[]{:S(2)}) async-start(bf16[1,2,32,1024]{3,2,0,1:T(8,128)(2,1)} %bitcast.21), calls=%async_computation.6 | async-start | bytes 262144 | tf_op jit(solution)/shard_map/all_to_all | solution.py:55
  19.6 4.9 %all-to-all-start.3 = ((bf16[8,2,4096]{2,1,0:T(2,128)(2,1)}), bf16[8,2,4096]{2,1,0:T(2,128)(2,1)S(1)}, u32[]{:S(2)}, u32[]{:S(2)}) async-start(bf16[8,2,4096]{2,1,0:T(2,128)(2,1)} %reshape.143), calls=%async_computation.3 | async-start | bytes 262144 | tf_op jit(solution)/shard_map/all_to_all | solution.py:47
  25.8 2.2 gather_fusion.2
  29.5 4.8 %all-to-all-start.7 = ((bf16[8,2,4096]{2,1,0:T(2,128)(2,1)}), bf16[8,2,4096]{2,1,0:T(2,128)(2,1)S(1)}, u32[]{:S(2)}, u32[]{:S(2)}) async-start(bf16[8,2,4096]{2,1,0:T(2,128)(2,1)} %reshape.147), calls=%async_computation.7 | async-start | bytes 262144 | tf_op jit(solution)/shard_map/all_to_all | solution.py:54
  34.3 2.4 broadcast_select_fusion
  36.8 2.2 all-to-all-done.7
  39.0 17.2 %all_to_all.81 = bf16[1,2,32,8192]{3,2,0,1:T(8,128)(2,1)} all-to-all(bf16[1,2,32,8192]{3,2,0,1:T(8,128)(2,1)S(1)} %bitcast.176), channel_id=1, replica_groups=mesh['dp'=2,'ctx'=16,'tp'=8] {'dp'}, dimensions={1} | all-to-all | bytes 2097152 | tf_op jit(solution)/shard_map/all_to_all | solution.py:41
  56.2 5.3 %all-to-all-start.4 = ((bf16[1,2,32,8192]{3,2,0,1:T(8,128)(2,1)}), bf16[1,2,32,8192]{3,2,0,1:T(8,128)(2,1)S(1)}, u32[]{:S(2)}, u32[]{:S(2)}) async-start(bf16[1,2,32,8192]{3,2,0,1:T(8,128)(2,1)} %bitcast.16), calls=%async_computation.4 | async-start | bytes 2097152 | tf_op jit(solution)/shard_map/all_to_all | solution.py:62
  61.5 9.1 %copy.60 = bf16[1,2,32,8192]{2,1,0,3:T(2,128)(2,1)} copy(bf16[1,2,32,8192]{3,2,0,1:T(8,128)(2,1)} %all_to_all.81) | data formatting | bytes 2097152 | tf_op jit(solution)/shard_map/all_to_all | solution.py:41
  70.6 7.8 %reshape.141 = bf16[8,2,32768]{2,1,0:T(2,128)(2,1)} reshape(bf16[8192,1,2,32]{3,2,1,0:T(2,128)(2,1)} %bitcast.170) | data formatting | bytes 2097152
  78.5 4.9 %all-to-all-start.1 = ((bf16[8,2,32768]{2,1,0:T(2,128)(2,1)}), bf16[8,2,32768]{2,1,0:T(2,128)(2,1)S(1)}, u32[]{:S(2)}, u32[]{:S(2)}) async-start(bf16[8,2,32768]{2,1,0:T(2,128)(2,1)} %reshape.141), calls=%async_computation.1 | async-start | bytes 2097152 | tf_op jit(solution)/shard_map/all_to_all | solution.py:40
  83.8 6.8 %copy.67 = bf16[1,2,32,8192]{2,1,0,3:T(2,128)(2,1)} copy(bf16[1,2,32,8192]{3,2,0,1:T(8,128)(2,1)S(1)} %all-to-all-done.4) | data formatting | bytes 2097152 | tf_op jit(solution)/shard_map/all_to_all | solution.py:62
  90.6 7.8 %reshape.145 = bf16[8,2,32768]{2,1,0:T(2,128)(2,1)} reshape(bf16[8192,1,2,32]{3,2,1,0:T(2,128)(2,1)} %bitcast.171) | data formatting | bytes 2097152
  98.4 5.1 %all-to-all-start.5 = ((bf16[8,2,32768]{2,1,0:T(2,128)(2,1)}), bf16[8,2,32768]{2,1,0:T(2,128)(2,1)}, u32[]{:S(2)}, u32[]{:S(2)}) async-start(bf16[8,2,32768]{2,1,0:T(2,128)(2,1)} %reshape.145), calls=%async_computation.5 | async-start | bytes 2097152 | tf_op jit(solution)/shard_map/all_to_all | solution.py:61
  104.7 3.8 %collective-permute-start = (bf16[512,128]{1,0:T(8,128)(2,1)S(1)}, bf16[512,128]{1,0:T(8,128)(2,1)S(1)}, u32[]{:S(2)}, u32[]{:S(2)}) collective-permute-start(bf16[512,128]{1,0:T(8,128)(2,1)S(1)} %bitcast.189), channel_id=1, source_target_pairs={{0,16},{8,24},{16,32},{24,40},{32,48},{40,56},{48,64},{56,72},{64,... | collective-permute-start | bytes 393224 | tf_op jit(solution)/shard_map/ppermute | solution.py:16
  108.6 4.1 %collective-permute-start.1 = (bf16[512,128]{1,0:T(8,128)(2,1)S(1)}, bf16[512,128]{1,0:T(8,128)(2,1)S(1)}, u32[]{:S(2)}, u32[]{:S(2)}) collective-permute-start(bf16[512,128]{1,0:T(8,128)(2,1)S(1)} %bitcast.190), channel_id=1, source_target_pairs={{0,8},{8,16},{16,24},{24,32},{32,40},{40,48},{48,56},{56,64},{64,7... | collective-permute-start | bytes 393224 | tf_op jit(solution)/shard_map/ppermute | solution.py:16
  113.9 3.8 %collective-permute-start.2 = (bf16[512,128]{1,0:T(8,128)(2,1)S(1)}, bf16[512,128]{1,0:T(8,128)(2,1)S(1)}, u32[]{:S(2)}, u32[]{:S(2)}) collective-permute-start(bf16[512,128]{1,0:T(8,128)(2,1)S(1)} %bitcast.192), channel_id=1, source_target_pairs={{0,16},{8,24},{16,32},{24,40},{32,48},{40,56},{48,64},{56,72},{64,... | collective-permute-start | bytes 393224 | tf_op jit(solution)/shard_map/ppermute | solution.py:16
  117.7 5.9 %collective-permute-start.3 = (bf16[512,128]{1,0:T(8,128)(2,1)S(1)}, bf16[512,128]{1,0:T(8,128)(2,1)S(1)}, u32[]{:S(2)}, u32[]{:S(2)}) collective-permute-start(bf16[512,128]{1,0:T(8,128)(2,1)S(1)} %bitcast.193), channel_id=1, source_target_pairs={{0,8},{8,16},{16,24},{24,32},{32,40},{40,48},{48,56},{56,64},{64,7... | collective-permute-start | bytes 393224 | tf_op jit(solution)/shard_map/ppermute | solution.py:16
  123.8 3.2 %collective-permute-done.3 = bf16[512,128]{1,0:T(8,128)(2,1)S(1)} collective-permute-done((bf16[512,128]{1,0:T(8,128)(2,1)S(1)}, bf16[512,128]{1,0:T(8,128)(2,1)S(1)}, u32[]{:S(2)}, u32[]{:S(2)}) %collective-permute-start.3) | collective-permute-done | bytes 131104 | tf_op jit(solution)/shard_map/ppermute | solution.py:16
  127.0 7.0 %reshape.142 = bf16[8192,1,2,32]{3,2,1,0:T(2,128)(2,1)} reshape(bf16[8,2,32768]{2,1,0:T(2,128)(2,1)} %copy-done.2) | data formatting | bytes 2097152
  134.1 7.1 %copy.78 = bf16[1,2,32,8,1024]{4,3,2,1,0:T(8,128)(2,1)} copy(bf16[1,2,32,8,1024]{2,1,4,3,0:T(2,128)(2,1)} %bitcast.172) | data formatting | bytes 2097152 | tf_op jit(solution)/shard_map/all_to_all | solution.py:40
  144.4 7.0 %reshape.146 = bf16[8192,1,2,32]{3,2,1,0:T(2,128)(2,1)} reshape(bf16[8,2,32768]{2,1,0:T(2,128)(2,1)} %all-to-all-done.5) | data formatting | bytes 2097152
  151.4 7.1 %copy.79 = bf16[1,2,32,8,1024]{4,3,2,1,0:T(8,128)(2,1)} copy(bf16[1,2,32,8,1024]{2,1,4,3,0:T(2,128)(2,1)} %bitcast.173) | data formatting | bytes 2097152 | tf_op jit(solution)/shard_map/all_to_all | solution.py:61
  161.6 2.5 copy.75
  164.2 92.4 %while.20 = (s32[]{:T(128)}, f32[1536,1,128]{2,0,1:T(8,128)S(1)}, f32[1536,1,128]{2,0,1:T(8,128)S(1)}, bf16[512,8,128]{0,2,1:T(8,128)(2,1)}, bf16[512,8,128]{2,0...) while((s32[]{:T(128)}, f32[1536,1,128]{2,0,1:T(8,128)S(1)}, ...), condition=%wide.region_7.10_spmd.clone, body=%wide.region_3.0_spmd.clone.sunk | while | flops 1221327360 | bytes 26379400 | solution.py:142
  257.5 3.2 %collective-permute-start.6 = (f32[512,128]{1,0:T(8,128)}, f32[512,128]{1,0:T(8,128)S(1)}, u32[]{:S(2)}, u32[]{:S(2)}) collective-permute-start(f32[512,128]{1,0:T(8,128)} %get-tuple-element.322), channel_id=1, source_target_pairs={{8,0},{16,8},{24,16},{32,24},{40,32},{48,40},{56,48},{64,56},{72,6... | collective-permute-start | bytes 786440 | tf_op jit(solution)/shard_map/ppermute | solution.py:16
  267.3 2.9 %copy.77 = bf16[512,8,128]{2,1,0:T(8,128)(2,1)} copy(bf16[512,8,128]{2,0,1:T(8,128)(2,1)} %get-tuple-element.179) | data formatting | bytes 2097152 | tf_op jit(solution)/shard_map/while | solution.py:142
  270.1 2.3 reshape.96
  272.4 2.3 copy.80
  274.7 2.1 collective-permute-done.7
  278.9 6.4 %collective-permute-done.5 = f32[512,128]{1,0:T(8,128)} collective-permute-done((f32[512,128]{1,0:T(8,128)}, f32[512,128]{1,0:T(8,128)}, u32[]{:S(2)}, u32[]{:S(2)}) %collective-permute-start.5) | collective-permute-done | bytes 262176 | tf_op jit(solution)/shard_map/ppermute | solution.py:16
  (135 shorter events, 123.2 us)
Async XLA Ops:
  0.6 23.9 %copy-start = (bf16[1,64,8192]{2,1,0:T(8,128)(2,1)S(1)}, bf16[1,64,8192]{2,1,0:T(8,128)(2,1)}, u32[]{:S(2)}) copy-start(bf16[1,64,8192]{2,1,0:T(8,128)(2,1)} %param.12) | copy-start | bytes 3145732
  11.8 7.9 %all-to-all-start.6 = ((bf16[1,2,32,1024]{3,2,0,1:T(8,128)(2,1)}), bf16[1,2,32,1024]{3,2,0,1:T(8,128)(2,1)S(1)}, u32[]{:S(2)}, u32[]{:S(2)}) async-start(bf16[1,2,32,1024]{3,2,0,1:T(8,128)(2,1)} %bitcast.21), calls=%async_computation.6 | async-start | bytes 262144 | tf_op jit(solution)/shard_map/all_to_all | solution.py:55
  19.6 9.9 %all-to-all-start.3 = ((bf16[8,2,4096]{2,1,0:T(2,128)(2,1)}), bf16[8,2,4096]{2,1,0:T(2,128)(2,1)S(1)}, u32[]{:S(2)}, u32[]{:S(2)}) async-start(bf16[8,2,4096]{2,1,0:T(2,128)(2,1)} %reshape.143), calls=%async_computation.3 | async-start | bytes 262144 | tf_op jit(solution)/shard_map/all_to_all | solution.py:47
  24.6 1.2 copy-start.1
  29.5 9.5 %all-to-all-start.7 = ((bf16[8,2,4096]{2,1,0:T(2,128)(2,1)}), bf16[8,2,4096]{2,1,0:T(2,128)(2,1)S(1)}, u32[]{:S(2)}, u32[]{:S(2)}) async-start(bf16[8,2,4096]{2,1,0:T(2,128)(2,1)} %reshape.147), calls=%async_computation.7 | async-start | bytes 262144 | tf_op jit(solution)/shard_map/all_to_all | solution.py:54
  56.2 22.3 %all-to-all-start.4 = ((bf16[1,2,32,8192]{3,2,0,1:T(8,128)(2,1)}), bf16[1,2,32,8192]{3,2,0,1:T(8,128)(2,1)S(1)}, u32[]{:S(2)}, u32[]{:S(2)}) async-start(bf16[1,2,32,8192]{3,2,0,1:T(8,128)(2,1)} %bitcast.16), calls=%async_computation.4 | async-start | bytes 2097152 | tf_op jit(solution)/shard_map/all_to_all | solution.py:62
  70.6 12.8 %copy-start.5 = (s32[1,32]{1,0:T(1,128)S(1)}, s32[1,32]{1,0:T(1,128)}, u32[]{:S(2)}) copy-start(s32[1,32]{1,0:T(1,128)} %param.17) | copy-start | bytes 388
  78.5 19.9 %all-to-all-start.1 = ((bf16[8,2,32768]{2,1,0:T(2,128)(2,1)}), bf16[8,2,32768]{2,1,0:T(2,128)(2,1)S(1)}, u32[]{:S(2)}, u32[]{:S(2)}) async-start(bf16[8,2,32768]{2,1,0:T(2,128)(2,1)} %reshape.141), calls=%async_computation.1 | async-start | bytes 2097152 | tf_op jit(solution)/shard_map/all_to_all | solution.py:40
  98.4 25.3 %copy-start.2 = (bf16[8,2,32768]{2,1,0:T(2,128)(2,1)}, bf16[8,2,32768]{2,1,0:T(2,128)(2,1)S(1)}, u32[]{:S(2)}) copy-start(bf16[8,2,32768]{2,1,0:T(2,128)(2,1)S(1)} %all-to-all-done.1) | copy-start | bytes 3145732
  98.4 45.9 %all-to-all-start.5 = ((bf16[8,2,32768]{2,1,0:T(2,128)(2,1)}), bf16[8,2,32768]{2,1,0:T(2,128)(2,1)}, u32[]{:S(2)}, u32[]{:S(2)}) async-start(bf16[8,2,32768]{2,1,0:T(2,128)(2,1)} %reshape.145), calls=%async_computation.5 | async-start | bytes 2097152 | tf_op jit(solution)/shard_map/all_to_all | solution.py:61
  104.7 19.0 %collective-permute-start = (bf16[512,128]{1,0:T(8,128)(2,1)S(1)}, bf16[512,128]{1,0:T(8,128)(2,1)S(1)}, u32[]{:S(2)}, u32[]{:S(2)}) collective-permute-start(bf16[512,128]{1,0:T(8,128)(2,1)S(1)} %bitcast.189), channel_id=1, source_target_pairs={{0,16},{8,24},{16,32},{24,40},{32,48},{40,56},{48,64},{56,72},{64,... | collective-permute-start | bytes 393224 | tf_op jit(solution)/shard_map/ppermute | solution.py:16
  108.6 15.1 %collective-permute-start.1 = (bf16[512,128]{1,0:T(8,128)(2,1)S(1)}, bf16[512,128]{1,0:T(8,128)(2,1)S(1)}, u32[]{:S(2)}, u32[]{:S(2)}) collective-permute-start(bf16[512,128]{1,0:T(8,128)(2,1)S(1)} %bitcast.190), channel_id=1, source_target_pairs={{0,8},{8,16},{16,24},{24,32},{32,40},{40,48},{48,56},{56,64},{64,7... | collective-permute-start | bytes 393224 | tf_op jit(solution)/shard_map/ppermute | solution.py:16
  113.9 9.8 %collective-permute-start.2 = (bf16[512,128]{1,0:T(8,128)(2,1)S(1)}, bf16[512,128]{1,0:T(8,128)(2,1)S(1)}, u32[]{:S(2)}, u32[]{:S(2)}) collective-permute-start(bf16[512,128]{1,0:T(8,128)(2,1)S(1)} %bitcast.192), channel_id=1, source_target_pairs={{0,16},{8,24},{16,32},{24,40},{32,48},{40,56},{48,64},{56,72},{64,... | collective-permute-start | bytes 393224 | tf_op jit(solution)/shard_map/ppermute | solution.py:16
  117.7 9.3 %collective-permute-start.3 = (bf16[512,128]{1,0:T(8,128)(2,1)S(1)}, bf16[512,128]{1,0:T(8,128)(2,1)S(1)}, u32[]{:S(2)}, u32[]{:S(2)}) collective-permute-start(bf16[512,128]{1,0:T(8,128)(2,1)S(1)} %bitcast.193), channel_id=1, source_target_pairs={{0,8},{8,16},{16,24},{24,32},{32,40},{40,48},{48,56},{56,64},{64,7... | collective-permute-start | bytes 393224 | tf_op jit(solution)/shard_map/ppermute | solution.py:16
  160.3 3.9 %copy-start.3 = (s32[1536]{0:T(1024)S(1)}, s32[1536]{0:T(1024)}, u32[]{:S(2)}) copy-start(s32[1536]{0:T(1024)} %broadcast_add_fusion) | copy-start | bytes 18436
  160.3 3.9 %copy-start.4 = (s32[512]{0:T(512)S(1)}, s32[512]{0:T(512)}, u32[]{:S(2)}) copy-start(s32[512]{0:T(512)} %broadcast_add_fusion.1) | copy-start | bytes 6148
  257.5 17.2 %collective-permute-start.6 = (f32[512,128]{1,0:T(8,128)}, f32[512,128]{1,0:T(8,128)S(1)}, u32[]{:S(2)}, u32[]{:S(2)}) collective-permute-start(f32[512,128]{1,0:T(8,128)} %get-tuple-element.322), channel_id=1, source_target_pairs={{8,0},{16,8},{24,16},{32,24},{40,32},{48,40},{56,48},{64,56},{72,6... | collective-permute-start | bytes 786440 | tf_op jit(solution)/shard_map/ppermute | solution.py:16
  260.7 16.1 %collective-permute-start.7 = (f32[512,128]{1,0:T(8,128)}, f32[512,128]{1,0:T(8,128)S(1)}, u32[]{:S(2)}, u32[]{:S(2)}) collective-permute-start(f32[512,128]{1,0:T(8,128)} %get-tuple-element.323), channel_id=1, source_target_pairs={{16,0},{24,8},{32,16},{40,24},{48,32},{56,40},{64,48},{72,56},{80,... | collective-permute-start | bytes 786440 | tf_op jit(solution)/shard_map/ppermute | solution.py:16
  263.4 15.5 %collective-permute-start.4 = (f32[512,128]{1,0:T(8,128)}, f32[512,128]{1,0:T(8,128)S(1)}, u32[]{:S(2)}, u32[]{:S(2)}) collective-permute-start(f32[512,128]{1,0:T(8,128)} %get-tuple-element.324), channel_id=1, source_target_pairs={{8,0},{16,8},{24,16},{32,24},{40,32},{48,40},{56,48},{64,56},{72,6... | collective-permute-start | bytes 786440 | tf_op jit(solution)/shard_map/ppermute | solution.py:16
  265.3 19.9 %collective-permute-start.5 = (f32[512,128]{1,0:T(8,128)}, f32[512,128]{1,0:T(8,128)}, u32[]{:S(2)}, u32[]{:S(2)}) collective-permute-start(f32[512,128]{1,0:T(8,128)} %get-tuple-element.325), channel_id=1, source_target_pairs={{16,0},{24,8},{32,16},{40,24},{48,32},{56,40},{64,48},{72,56},{80,... | collective-permute-start | bytes 786440 | tf_op jit(solution)/shard_map/ppermute | solution.py:16
where the time goes:
time: 290 us; the launch traced here: 287 us
  local copies, waits for them, and re-layouts  94.2 us (32%)
  matrix products  77.4 us (27%)
  starting transfers between devices  57.1 us (20%)
  blocking collectives  22.7 us (8%)
  other arithmetic  17.9 us (6%)
  waiting for transfers between devices  16.3 us (6%)
    unnamed x24, local copies, waits for them, and re-layouts  37.8 us
    ppermute x8, starting transfers between devices, shifted(): return lax.ppermute(block, axis, route)  26.7 us
    all_to_all x1, blocking collectives, on_device(): lax.all_to_all(query_sent, 'dp', split_axis=1, concat_axis=1, tiled=True)  17.2 us
    dot_general x8, matrix products, head_step(): jnp.einsum('qd,kd->qk', query_head, key_head, preferred_element_type=jnp....  15.1 us
    dot_general x8, matrix products, head_step(): jnp.einsum('qd,kd->qk', grad_head, value_head, preferred_element_type=jnp...  13.6 us
    ppermute x8, waiting for transfers between devices, shifted(): return lax.ppermute(block, axis, route)  13.1 us
    dot_general x8, matrix products, head_step(): jnp.einsum('qk,qd->kd', dscore, query_head, preferred_element_type=jnp.fl...  13.1 us
    dot_general x8, matrix products, head_step(): jnp.einsum('qk,qd->kd', prob, grad_head, preferred_element_type=jnp.float32)  13 us
  transfers between devices with their start and end apart: 14, of which 6 were waited for; matrix products, arithmetic and copies ran while one was open for 24% of the time, Pallas kernels for 0%

commit v1 on v0

v1 whole, which is shorter than its diff:
```python
import functools
import math

import jax
import jax.numpy as jnp
from jax import lax
from jax.experimental import pallas as pl
from jax.experimental.pallas import tpu as pltpu
from jax.sharding import PartitionSpec as P

HD = 128
SPAN = 2
FIRST_HEADS = 4
STEP_HEADS = 2
TILE = 256
SCALE = 1.0 / math.sqrt(HD)
LOG2_SCALE = math.log2(math.e) * SCALE
NT = (((1,), (1,)), ((), ()))
NN = (((1,), (0,)), ((), ()))
TN = (((0,), (0,)), ((), ()))


def dot(a, b, dims):
    return lax.dot_general(a, b, dims, preferred_element_type=jnp.float32)


def pack_kernel(heads, first, order_ref, q_ref, k_ref, v_ref, g_ref, one_ref, two_ref):
    rows = q_ref.shape[0]
    group = rows // one_ref.shape[0]
    row = lax.broadcasted_iota(jnp.int32, (rows, rows), 0)
    pick = (row == order_ref[...]).astype(jnp.bfloat16)
    cut = first * HD

    def put(ref, begin, block):
        moved = dot(pick, block, TN).astype(jnp.bfloat16)
        for replica in range(ref.shape[0]):
            ref[replica, :, begin : begin + block.shape[1]] = moved[
                replica * group : (replica + 1) * group
            ]

    put(one_ref, 0, k_ref[...])
    put(one_ref, HD, v_ref[...])
    put(one_ref, 2 * HD, q_ref[:, :cut])
    put(one_ref, 2 * HD + cut, g_ref[:, :cut])
    put(two_ref, 0, q_ref[:, cut:])
    put(two_ref, heads * HD - cut, g_ref[:, cut:])


def pack(order, queries, key_rows, values_in, out_grad, replicas, slots, first):
    rows = queries.shape[0]
    heads = queries.shape[1] // slots // HD
    wide = pl.BlockSpec((rows, heads * HD), lambda t: (0, t))
    thin = pl.BlockSpec((rows, HD), lambda t: (0, t))
    widths = (2 * HD + 2 * first * HD, 2 * (heads - first) * HD)
    return pl.pallas_call(
        functools.partial(pack_kernel, heads, first),
        grid=(slots,),
        in_specs=[pl.BlockSpec((1, rows), lambda t: (0, 0)), wide, thin, thin, wide],
        out_specs=[
            pl.BlockSpec((replicas, rows // replicas, w), lambda t: (t, 0, 0)) for w in widths
        ],
        out_shape=[
            jax.ShapeDtypeStruct((slots * replicas, rows // replicas, w), jnp.bfloat16)
            for w in widths
        ],
        compiler_params=pltpu.CompilerParams(vmem_limit_bytes=32 * 2**20),
    )(order, queries, key_rows, values_in, out_grad)


def fill_bias(lengths_ref, bias_ref):
    block_rows = bias_ref.shape[0]
    margin = SPAN * block_rows
    docs = lengths_ref.shape[1]
    lengths = lengths_ref[...].astype(jnp.float32)
    down = lax.broadcasted_iota(jnp.int32, (docs, docs), 0)
    across = lax.broadcasted_iota(jnp.int32, (docs, docs), 1)
    column = jnp.sum(jnp.where(down == across, lengths, 0.0), axis=1, keepdims=True)
    starts = jnp.sum(jnp.where(down < across, column, 0.0), axis=0, keepdims=True)
    first = lax.axis_index("ctx") * block_rows
    place = first + lax.broadcasted_iota(jnp.int32, (block_rows, docs), 0)
    begun = starts <= place.astype(jnp.float32)
    begin = jnp.max(jnp.where(begun, starts, 0.0), axis=1, keepdims=True).astype(jnp.int32)
    begin = begin - (first - margin)
    for t in range(block_rows // TILE):
        here = slice(t * TILE, (t + 1) * TILE)
        row = lax.broadcasted_iota(jnp.int32, (TILE, margin + TILE), 0)
        col = lax.broadcasted_iota(jnp.int32, (TILE, margin + TILE), 1)
        allowed = (col <= row + margin) & (col >= begin[here] - t * TILE)
        bias_ref[here, :] = jnp.where(allowed, 0.0, -1e30)


def one_head(cols, q_ref, g_ref, key_win, value_win, bias_ref, out_ref, dq_ref, dk_ref, dv_ref):
    block_rows = q_ref.shape[0]
    margin = SPAN * block_rows
    for t in range(block_rows // TILE):
        here = slice(t * TILE, (t + 1) * TILE)
        window = slice(t * TILE, (t + 1) * TILE + margin)
        query, grad = q_ref[here, cols], g_ref[here, cols]
        key, value = key_win[window, :], value_win[window, :]
        scores = dot(query, key, NT) * LOG2_SCALE + bias_ref[here, :]
        top = jnp.max(scores, axis=1, keepdims=True)
        expo = jnp.exp2(scores - top)
        inverse = 1.0 / jnp.sum(expo, axis=1, keepdims=True)
        prob = expo.astype(jnp.bfloat16)
        output = (dot(prob, value, NN) * inverse).astype(jnp.bfloat16)
        out_ref[here, cols] = output
        grad = (grad.astype(jnp.float32) * inverse).astype(jnp.bfloat16)
        delta = jnp.sum(
            grad.astype(jnp.float32) * output.astype(jnp.float32), axis=1, keepdims=True
        )
        dprob = dot(grad, value, NT)
        dscore = (prob.astype(jnp.float32) * (dprob - delta)).astype(jnp.bfloat16)
        dq_ref[here, cols] = (dot(dscore, key, NN) * SCALE).astype(jnp.bfloat16)
        dv_ref[:, window] += dot(grad, prob, TN)
        dk_ref[:, window] += dot(query, dscore, TN)


def gather_window(k_ref, v_ref, kv1_ref, kv2_ref, key_win, value_win):
    block_rows = k_ref.shape[0]
    for place, ref in ((0, kv2_ref), (1, kv1_ref)):
        here = slice(place * block_rows, (place + 1) * block_rows)
        key_win[here, :] = ref[:, :HD]
        value_win[here, :] = ref[:, HD:]
    key_win[SPAN * block_rows :, :] = k_ref[...]
    value_win[SPAN * block_rows :, :] = v_ref[...]


def first_kernel(
    lengths_ref, q_ref, g_ref, k_ref, v_ref, kv1_ref, kv2_ref,
    out_ref, dq_ref, dk_ref, dv_ref,
    key_win, value_win, bias_ref,
):
    @pl.when(pl.program_id(0) == 0)
    def _():
        gather_window(k_ref, v_ref, kv1_ref, kv2_ref, key_win, value_win)
        fill_bias(lengths_ref, bias_ref)
        dk_ref[...] = jnp.zeros_like(dk_ref)
        dv_ref[...] = jnp.zeros_like(dv_ref)

    for head in range(STEP_HEADS):
        one_head(
            slice(head * HD, (head + 1) * HD),
            q_ref, g_ref, key_win, value_win, bias_ref, out_ref, dq_ref, dk_ref, dv_ref,
        )


def second_kernel(
    lengths_ref, q_ref, g_ref, k_ref, v_ref, kv1_ref, kv2_ref, dk_in, dv_in, out_in, dq_in,
    out_ref, dq_ref, own_ref, back1_ref, back2_ref,
    key_win, value_win, bias_ref, dk_ref, dv_ref,
):
    @pl.when(pl.program_id(0) == 0)
    def _():
        gather_window(k_ref, v_ref, kv1_ref, kv2_ref, key_win, value_win)
        fill_bias(lengths_ref, bias_ref)
        dk_ref[...] = dk_in[...]
        dv_ref[...] = dv_in[...]

    for head in range(STEP_HEADS):
        one_head(
            slice(head * HD, (head + 1) * HD),
            q_ref, g_ref, key_win, value_win, bias_ref, out_ref, dq_ref, dk_ref, dv_ref,
        )

    @pl.when(pl.program_id(0) == pl.num_programs(0) - 1)
    def _():
        block_rows = q_ref.shape[0]
        for place, ref in ((0, back2_ref), (1, back1_ref), (2, own_ref)):
            here = slice(place * block_rows, (place + 1) * block_rows)
            ref[:, :HD] = (dk_ref[:, here] * SCALE).T.astype(ref.dtype)
            ref[:, HD:] = dv_ref[:, here].T.astype(ref.dtype)


def attend(one, two, back1, back2, lengths, heads, first):
    block_rows = one.shape[0]
    width = (SPAN + 1) * block_rows
    step = STEP_HEADS * HD
    whole = lambda shape: pl.BlockSpec(shape, lambda h: (0, 0))
    columns = lambda begin: pl.BlockSpec((block_rows, step), lambda h: (0, begin + h))
    key_part = pl.BlockSpec((block_rows, HD), lambda h: (0, 0))
    value_part = pl.BlockSpec((block_rows, HD), lambda h: (0, 1))
    pair = (block_rows, 2 * HD)
    out = jax.ShapeDtypeStruct((block_rows, heads * HD), jnp.bfloat16)
    total = jax.ShapeDtypeStruct((HD, width), jnp.float32)
    params = pltpu.CompilerParams(vmem_limit_bytes=40 * 2**20)
    window = [
        pltpu.VMEM((width, HD), jnp.bfloat16),
        pltpu.VMEM((width, HD), jnp.bfloat16),
        pltpu.VMEM((block_rows, SPAN * block_rows + TILE), jnp.float32),
    ]
    lead = 2 * HD // step
    attended, query_grad, dk, dv = pl.pallas_call(
        first_kernel,
        grid=(first // STEP_HEADS,),
        in_specs=[
            whole(lengths.shape),
            columns(lead), columns(lead + first // STEP_HEADS),
            key_part, value_part, whole(pair), whole(pair),
        ],
        out_specs=[columns(0), columns(0), whole(total.shape), whole(total.shape)],
        out_shape=[out, out, total, total],
        scratch_shapes=window,
        compiler_params=params,
    )(lengths, one, one, one, one, back1, back2)
    rest = heads - first
    begin = first // STEP_HEADS
    return pl.pallas_call(
        second_kernel,
        grid=(rest // STEP_HEADS,),
        in_specs=[
            whole(lengths.shape),
            columns(0), columns(rest // STEP_HEADS),
            key_part, value_part, whole(pair), whole(pair),
            whole(total.shape), whole(total.shape),
            pl.BlockSpec(memory_space=pl.ANY), pl.BlockSpec(memory_space=pl.ANY),
        ],
        out_specs=[columns(begin), columns(begin), whole(pair), whole(pair), whole(pair)],
        out_shape=[
            out, out,
            jax.ShapeDtypeStruct(pair, jnp.float32),
            jax.ShapeDtypeStruct(pair, jnp.bfloat16),
            jax.ShapeDtypeStruct(pair, jnp.bfloat16),
        ],
        scratch_shapes=window + [
            pltpu.VMEM(total.shape, jnp.float32), pltpu.VMEM(total.shape, jnp.float32)
        ],
        input_output_aliases={9: 0, 10: 1},
        compiler_params=params,
    )(lengths, two, two, one, one, back1, back2, dk, dv, attended, query_grad)


def shifted(block, axis, distance):
    devices = range(lax.axis_size(axis))
    route = [(i - distance, i) for i in devices if i - distance in devices]
    return lax.ppermute(block, axis, route)


def exchange(block):
    return lax.all_to_all(block, ("tp", "dp"), split_axis=0, concat_axis=0, tiled=True)


def on_device(queries, key_rows, values_in, out_grad, send_rows, doc_lengths):
    replicas, slots = lax.axis_size("dp"), lax.axis_size("tp")
    heads = queries.shape[2] // slots // HD
    one, two = pack(
        send_rows[0], queries[0], key_rows[0], values_in[0], out_grad[0], replicas, slots, FIRST_HEADS
    )
    one = exchange(one)
    one = one.reshape(one.shape[0] * one.shape[1], one.shape[2])
    key_value = one[:, : 2 * HD]
    previous = [shifted(key_value, "ctx", offset) for offset in range(1, SPAN + 1)]
    two = exchange(two)
    two = two.reshape(two.shape[0] * two.shape[1], two.shape[2])
    attended, query_grad, own, back1, back2 = attend(
        one, two, previous[0], previous[1], doc_lengths, heads, FIRST_HEADS
    )
    for offset, part in ((2, back2), (1, back1)):
        own = own + shifted(part, "ctx", -offset).astype(jnp.float32)
    own = own.astype(jnp.bfloat16)
    return (attended[None], query_grad[None], own[None, :, :HD], own[None, :, HD:])


def solution(mesh):
    rows = P("dp", ("ctx", "tp"), None)
    out = P("dp", "ctx", "tp")
    return jax.shard_map(
        on_device,
        mesh=mesh,
        in_specs=(rows, rows, rows, rows, rows, P("dp", None)),
        out_specs=(out, out, out, out),
        check_vma=False,
    )
```

time: 290 us -> 102 us (0.35)
  the two profiles are of different devices: /device:TPU:42 before, /device:TPU:102 now
where the time goes in v1:
time: 102 us
  Pallas kernels  27.3 us (27%)
  blocking collectives  23.8 us (23%)
  waiting for transfers between devices  23.2 us (23%)
  starting transfers between devices  17.1 us (17%)
  local copies, waits for them, and re-layouts  9.72 us (10%)
    all_to_all x1, blocking collectives, exchange(): lax.all_to_all(block, ('tp', 'dp'), split_axis=0, concat_axis=0, tiled=True)  23.8 us
    ppermute x4, waiting for transfers between devices, shifted(): return lax.ppermute(block, axis, route)  23.2 us
    ppermute x4, starting transfers between devices, shifted(): return lax.ppermute(block, axis, route)  12.7 us
    pallas_call x1, Pallas kernels, attend(): pl.pallas_call(second_kernel, grid=(rest // STEP_HEADS,), in_specs=[whole...  11.9 us
    pallas_call x1, Pallas kernels, attend(): pl.pallas_call(first_kernel, grid=(first // STEP_HEADS,), in_specs=[whole...  11.3 us
    unnamed x20, local copies, waits for them, and re-layouts  8.98 us
    all_to_all x1, starting transfers between devices, exchange(): lax.all_to_all(block, ('tp', 'dp'), split_axis=0, concat_axis=0, tiled=True)  4.33 us
    pallas_call x1, Pallas kernels, pack(): pl.pallas_call(functools.partial(pack_kernel, heads, first), grid=(slots,...  4.11 us
  transfers between devices with their start and end apart: 5, of which 4 were waited for; matrix products, arithmetic and copies ran while one was open for 0% of the time, Pallas kernels for 11%

profile of v1, /device:TPU:102, one launch (start us, length us, event | category | flops | bytes accessed | tf_op | source)
XLA Modules:
  0.0 101.8 jit_solution(14043340002007261434)
XLA Ops:
  0.6 0.0 copy-start
  0.6 1.2 %copy-done = bf16[1,64,8192]{2,1,0:T(8,128)(2,1)S(1)} copy-done((bf16[1,64,8192]{2,1,0:T(8,128)(2,1)S(1)}, bf16[1,64,8192]{2,1,0:T(8,128)(2,1)}, u32[]{:S(2)}) %copy-start) | copy-done | bytes 1048600
  1.9 0.0 copy-start.1
  1.9 1.2 %copy-done.1 = bf16[1,64,8192]{2,1,0:T(8,128)(2,1)S(1)} copy-done((bf16[1,64,8192]{2,1,0:T(8,128)(2,1)S(1)}, bf16[1,64,8192]{2,1,0:T(8,128)(2,1)}, u32[]{:S(2)}) %copy-start.1) | copy-done | bytes 1048600
  3.1 0.0 copy-start.6
  3.1 0.9 copy-done.6
  4.0 0.0 copy-start.7
  4.0 0.9 copy-done.7
  4.9 0.0 copy-start.9
  4.9 0.7 copy-done.9
  5.5 4.1 %shard_map.93 = (bf16[16,32,1280]{2,1,0:T(8,128)(2,1)S(1)}, bf16[16,32,1024]{2,1,0:T(8,128)(2,1)}) custom-call(s32[1,64]{1,0:T(1,128)S(1)} %bitcast.26, bf16[64,8192]{1,0:T(8,128)(2,1)S(1)} %bitcast.22, bf16[64,1024]{1,0:T(8,128)(2,1)S(1)} %bitcast.24, bf16[64,1024]{1,0:T(8,128)(2,1)S(1)} %bitcast.25, bf16[64,8192]{1,0:T(8,128)(2,1)S(1)} %bitcast.23), custom_call_target="tpu_custom_call" | custom-call | tf_op jit(solution)/shard_map/pallas_call | solution.py:55
  9.7 23.8 %all_to_all.10 = bf16[16,32,1280]{2,1,0:T(8,128)(2,1)S(1)} all-to-all(bf16[16,32,1280]{2,1,0:T(8,128)(2,1)S(1)} %get-tuple-element.16), channel_id=1, replica_groups=mesh['dp'=2,'ctx'=16,'tp'=8] {'tp','dp'}, dimensions={0} | all-to-all | bytes 2621440 | tf_op jit(solution)/shard_map/all_to_all | solution.py:239
  33.4 0.0 copy-start.8
  33.4 4.3 %all-to-all-start = ((bf16[16,32,1024]{2,1,0:T(8,128)(2,1)}), bf16[16,32,1024]{2,1,0:T(8,128)(2,1)S(1)}, u32[]{:S(2)}, u32[]{:S(2)}) async-start(bf16[16,32,1024]{2,1,0:T(8,128)(2,1)} %get-tuple-element.15), calls=%async_computation | async-start | bytes 2097152 | tf_op jit(solution)/shard_map/all_to_all | solution.py:239
  37.8 5.0 %collective-permute-start.1 = (bf16[512,256]{1,0:T(8,128)(2,1)S(1)}, bf16[512,256]{1,0:T(8,128)(2,1)S(1)}, u32[]{:S(2)}, u32[]{:S(2)}) collective-permute-start(bf16[512,256]{1,0:T(8,128)(2,1)S(1)} %slice.12), channel_id=1, source_target_pairs={{0,16},{8,24},{16,32},{24,40},{32,48},{40,56},{48,64},{56,72},{64,... | collective-permute-start | bytes 786440 | tf_op jit(solution)/shard_map/ppermute | solution.py:235
  42.8 3.8 %collective-permute-start = (bf16[512,256]{1,0:T(8,128)(2,1)S(1)}, bf16[512,256]{1,0:T(8,128)(2,1)S(1)}, u32[]{:S(2)}, u32[]{:S(2)}) collective-permute-start(bf16[512,256]{1,0:T(8,128)(2,1)S(1)} %slice.12), channel_id=1, source_target_pairs={{0,8},{8,16},{16,24},{24,32},{32,40},{40,48},{48,56},{56,64},{64,7... | collective-permute-start | bytes 786440 | tf_op jit(solution)/shard_map/ppermute | solution.py:235
  46.6 2.9 %collective-permute-done.1.kv2_ref = bf16[512,256]{1,0:T(8,128)(2,1)S(1)} collective-permute-done((bf16[512,256]{1,0:T(8,128)(2,1)S(1)}, bf16[512,256]{1,0:T(8,128)(2,1)S(1)}, u32[]{:S(2)}, u32[]{:S(2)}) %collective-permute-start.1) | collective-permute-done | bytes 262176 | tf_op jit(solution)/shard_map/ppermute | solution.py:235
  49.5 7.7 %collective-permute-done.kv1_ref = bf16[512,256]{1,0:T(8,128)(2,1)S(1)} collective-permute-done((bf16[512,256]{1,0:T(8,128)(2,1)S(1)}, bf16[512,256]{1,0:T(8,128)(2,1)S(1)}, u32[]{:S(2)}, u32[]{:S(2)}) %collective-permute-start) | collective-permute-done | bytes 262176 | tf_op jit(solution)/shard_map/ppermute | solution.py:235
  57.2 0.0 copy-done.8
  57.2 11.3 %shard_map.94 = (bf16[512,1024]{1,0:T(8,128)(2,1)}, bf16[512,1024]{1,0:T(8,128)(2,1)}, f32[128,1536]{1,0:T(8,128)S(1)}, f32[128,1536]{1,0:T(8,128)S(1)}) custom-call(s32[1,32]{1,0:T(1,128)S(1)} %copy-done.8, bf16[512,1280]{1,0:T(8,128)(2,1)S(1)} %bitcast.14, bf16[512,1280]{1,0:T(8,128)(2,1)S(1)} %bitcast.15, bf16[512,1280]{1,0:T(8,128)(2,1)S(1)} %bitcast.16, ...), custom_call_target="tpu_custom_call" | custom-call | tf_op jit(solution)/shard_map/pallas_call | solution.py:192
  68.5 0.9 copy-done.2
  69.4 0.9 copy-done.4
  70.3 0.0 all-to-all-done
  70.3 1.1 %copy-done.3 = f32[128,1536]{1,0:T(8,128)S(1)} copy-done((f32[128,1536]{1,0:T(8,128)S(1)}, f32[128,1536]{1,0:T(8,128)}, u32[]{:S(2)}) %copy-start.3) | copy-done | bytes 786456
  71.4 1.1 %copy-done.5 = f32[128,1536]{1,0:T(8,128)S(1)} copy-done((f32[128,1536]{1,0:T(8,128)S(1)}, f32[128,1536]{1,0:T(8,128)}, u32[]{:S(2)}) %copy-start.5) | copy-done | bytes 786456
  72.6 11.9 %shard_map.95 = (bf16[512,1024]{1,0:T(8,128)(2,1)}, bf16[512,1024]{1,0:T(8,128)(2,1)}, f32[512,256]{1,0:T(8,128)S(1)}, bf16[512,256]{1,0:T(8,128)(2,1)S(1)}, bf16[512,256]{1,0:T(8,128)(2,1)S(1)}) custom-call(s32[1,32]{1,0:T(1,128)S(1)} %copy-done.8, bf16[512,1024]{1,0:T(8,128)(2,1)S(1)} %bitcast.20, ...), custom_call_target="tpu_custom_call", output_to_operand_aliasing={{0}: (9, {}), {1}: (10, {})} | custom-call | tf_op jit(solution)/shard_map/pallas_call | solution.py:207
  84.4 2.0 %collective-permute-start.2 = (bf16[512,256]{1,0:T(8,128)(2,1)S(1)}, bf16[512,256]{1,0:T(8,128)(2,1)S(1)}, u32[]{:S(2)}, u32[]{:S(2)}) collective-permute-start(bf16[512,256]{1,0:T(8,128)(2,1)S(1)} %get-tuple-element.24), channel_id=1, source_target_pairs={{16,0},{24,8},{32,16},{40,24},{48,32},{56,40},{64,48},{72,56},{80,... | collective-permute-start | bytes 786440 | tf_op jit(solution)/shard_map/ppermute | solution.py:235
  86.5 1.9 %collective-permute-start.3 = (bf16[512,256]{1,0:T(8,128)(2,1)S(1)}, bf16[512,256]{1,0:T(8,128)(2,1)S(1)}, u32[]{:S(2)}, u32[]{:S(2)}) collective-permute-start(bf16[512,256]{1,0:T(8,128)(2,1)S(1)} %get-tuple-element.25), channel_id=1, source_target_pairs={{8,0},{16,8},{24,16},{32,24},{40,32},{48,40},{56,48},{64,56},{72,6... | collective-permute-start | bytes 786440 | tf_op jit(solution)/shard_map/ppermute | solution.py:235
  88.4 7.2 %collective-permute-done.2 = bf16[512,256]{1,0:T(8,128)(2,1)S(1)} collective-permute-done((bf16[512,256]{1,0:T(8,128)(2,1)S(1)}, bf16[512,256]{1,0:T(8,128)(2,1)S(1)}, u32[]{:S(2)}, u32[]{:S(2)}) %collective-permute-start.2) | collective-permute-done | bytes 262176 | tf_op jit(solution)/shard_map/ppermute | solution.py:235
  95.6 5.4 %collective-permute-done.3 = bf16[512,256]{1,0:T(8,128)(2,1)S(1)} collective-permute-done((bf16[512,256]{1,0:T(8,128)(2,1)S(1)}, bf16[512,256]{1,0:T(8,128)(2,1)S(1)}, u32[]{:S(2)}, u32[]{:S(2)}) %collective-permute-start.3) | collective-permute-done | bytes 262176 | tf_op jit(solution)/shard_map/ppermute | solution.py:235
  101.0 0.1 add_convert_fusion
  101.0 0.7 slice_bitcast_fusion
  (5 shorter events, 0.0 us)
Async XLA Ops:
  0.6 1.2 %copy-start = (bf16[1,64,8192]{2,1,0:T(8,128)(2,1)S(1)}, bf16[1,64,8192]{2,1,0:T(8,128)(2,1)}, u32[]{:S(2)}) copy-start(bf16[1,64,8192]{2,1,0:T(8,128)(2,1)} %param.6) | copy-start | bytes 3145732
  1.9 1.2 %copy-start.1 = (bf16[1,64,8192]{2,1,0:T(8,128)(2,1)S(1)}, bf16[1,64,8192]{2,1,0:T(8,128)(2,1)}, u32[]{:S(2)}) copy-start(bf16[1,64,8192]{2,1,0:T(8,128)(2,1)} %param.9) | copy-start | bytes 3145732
  3.1 0.9 copy-start.6
  4.0 0.9 copy-start.7
  4.9 0.7 copy-start.9
  33.4 23.8 %copy-start.8 = (s32[1,32]{1,0:T(1,128)S(1)}, s32[1,32]{1,0:T(1,128)}, u32[]{:S(2)}) copy-start(s32[1,32]{1,0:T(1,128)} %lengths_ref.3) | copy-start | bytes 388
  33.4 36.9 %all-to-all-start = ((bf16[16,32,1024]{2,1,0:T(8,128)(2,1)}), bf16[16,32,1024]{2,1,0:T(8,128)(2,1)S(1)}, u32[]{:S(2)}, u32[]{:S(2)}) async-start(bf16[16,32,1024]{2,1,0:T(8,128)(2,1)} %get-tuple-element.15), calls=%async_computation | async-start | bytes 2097152 | tf_op jit(solution)/shard_map/all_to_all | solution.py:239
  37.8 11.7 %collective-permute-start.1 = (bf16[512,256]{1,0:T(8,128)(2,1)S(1)}, bf16[512,256]{1,0:T(8,128)(2,1)S(1)}, u32[]{:S(2)}, u32[]{:S(2)}) collective-permute-start(bf16[512,256]{1,0:T(8,128)(2,1)S(1)} %slice.12), channel_id=1, source_target_pairs={{0,16},{8,24},{16,32},{24,40},{32,48},{40,56},{48,64},{56,72},{64,... | collective-permute-start | bytes 786440 | tf_op jit(solution)/shard_map/ppermute | solution.py:235
  42.8 14.4 %collective-permute-start = (bf16[512,256]{1,0:T(8,128)(2,1)S(1)}, bf16[512,256]{1,0:T(8,128)(2,1)S(1)}, u32[]{:S(2)}, u32[]{:S(2)}) collective-permute-start(bf16[512,256]{1,0:T(8,128)(2,1)S(1)} %slice.12), channel_id=1, source_target_pairs={{0,8},{8,16},{16,24},{24,32},{32,40},{40,48},{48,56},{56,64},{64,7... | collective-permute-start | bytes 786440 | tf_op jit(solution)/shard_map/ppermute | solution.py:235
  68.5 0.9 copy-start.2
  69.4 0.9 copy-start.4
  70.3 1.1 %copy-start.3 = (f32[128,1536]{1,0:T(8,128)S(1)}, f32[128,1536]{1,0:T(8,128)}, u32[]{:S(2)}) copy-start(f32[128,1536]{1,0:T(8,128)} %copy-done.2) | copy-start | bytes 2359300
  71.4 1.1 %copy-start.5 = (f32[128,1536]{1,0:T(8,128)S(1)}, f32[128,1536]{1,0:T(8,128)}, u32[]{:S(2)}) copy-start(f32[128,1536]{1,0:T(8,128)} %copy-done.4) | copy-start | bytes 2359300
  84.4 11.1 %collective-permute-start.2 = (bf16[512,256]{1,0:T(8,128)(2,1)S(1)}, bf16[512,256]{1,0:T(8,128)(2,1)S(1)}, u32[]{:S(2)}, u32[]{:S(2)}) collective-permute-start(bf16[512,256]{1,0:T(8,128)(2,1)S(1)} %get-tuple-element.24), channel_id=1, source_target_pairs={{16,0},{24,8},{32,16},{40,24},{48,32},{56,40},{64,48},{72,56},{80,... | collective-permute-start | bytes 786440 | tf_op jit(solution)/shard_map/ppermute | solution.py:235
  86.5 14.5 %collective-permute-start.3 = (bf16[512,256]{1,0:T(8,128)(2,1)S(1)}, bf16[512,256]{1,0:T(8,128)(2,1)S(1)}, u32[]{:S(2)}, u32[]{:S(2)}) collective-permute-start(bf16[512,256]{1,0:T(8,128)(2,1)S(1)} %get-tuple-element.25), channel_id=1, source_target_pairs={{8,0},{16,8},{24,16},{32,24},{40,32},{48,40},{56,48},{64,56},{72,6... | collective-permute-start | bytes 786440 | tf_op jit(solution)/shard_map/ppermute | solution.py:235

commit v2 on v1

v2 whole, which is shorter than its diff:
```python
import functools
import math

import jax
import jax.numpy as jnp
from jax import lax
from jax.experimental import pallas as pl
from jax.experimental.pallas import tpu as pltpu
from jax.sharding import PartitionSpec as P

HD = 128
SPAN = 2
FIRST_HEADS = 5
PACK_SLOTS = 2
TILE = 256
SCALE = 1.0 / math.sqrt(HD)
LOG2_SCALE = math.log2(math.e) * SCALE
NT = (((1,), (1,)), ((), ()))
NN = (((1,), (0,)), ((), ()))
TN = (((0,), (0,)), ((), ()))


def dot(a, b, dims):
    return lax.dot_general(a, b, dims, preferred_element_type=jnp.float32)


def select(order_ref):
    rows = order_ref.shape[1]
    row = lax.broadcasted_iota(jnp.int32, (rows, rows), 0)
    return (row == order_ref[...]).astype(jnp.bfloat16)


def put(ref, slot, begin, moved):
    group = ref.shape[1]
    replicas = moved.shape[0] // group
    for replica in range(replicas):
        ref[slot * replicas + replica, :, begin : begin + moved.shape[1]] = moved[
            replica * group : (replica + 1) * group
        ]


def pack_small_kernel(order_ref, k_ref, v_ref, sent_ref):
    pick = select(order_ref)
    for begin, ref in ((0, k_ref), (HD, v_ref)):
        moved = dot(pick, ref[...], TN).astype(jnp.bfloat16)
        for slot in range(moved.shape[1] // HD):
            put(sent_ref, slot, begin, moved[:, slot * HD : (slot + 1) * HD])


def pack_large_kernel(heads, first, order_ref, q_ref, g_ref, one_ref, two_ref):
    pick = select(order_ref)
    cut = first * HD
    for index, ref in enumerate((q_ref, g_ref)):
        for slot in range(ref.shape[1] // (heads * HD)):
            begin = slot * heads * HD
            moved = dot(pick, ref[:, begin : begin + heads * HD], TN).astype(jnp.bfloat16)
            put(one_ref, slot, index * cut, moved[:, :cut])
            put(two_ref, slot, index * (heads * HD - cut), moved[:, cut:])


def in_hbm(*arrays):
    return [pltpu.with_memory_space_constraint(a, pltpu.HBM) for a in arrays]


def pack_small(order, key_rows, values_in, replicas, slots):
    rows, columns = key_rows.shape
    whole = lambda shape: pl.BlockSpec(shape, lambda: (0,) * len(shape))
    sent = (slots * replicas, rows // replicas, 2 * columns // slots)
    return pl.pallas_call(
        pack_small_kernel,
        in_specs=[whole(order.shape), whole(key_rows.shape), whole(values_in.shape)],
        out_specs=whole(sent),
        out_shape=jax.ShapeDtypeStruct(sent, jnp.bfloat16),
        compiler_params=pltpu.CompilerParams(vmem_limit_bytes=16 * 2**20),
    )(*in_hbm(order, key_rows, values_in))


def pack_large(order, queries, out_grad, replicas, slots, first):
    rows, columns = queries.shape
    heads = columns // slots // HD
    wide = pl.BlockSpec((rows, PACK_SLOTS * heads * HD), lambda t: (0, t))
    widths = (2 * first * HD, 2 * (heads - first) * HD)
    return pl.pallas_call(
        functools.partial(pack_large_kernel, heads, first),
        grid=(slots // PACK_SLOTS,),
        in_specs=[pl.BlockSpec(order.shape, lambda t: (0, 0)), wide, wide],
        out_specs=[
            pl.BlockSpec((PACK_SLOTS * replicas, rows // replicas, w), lambda t: (t, 0, 0))
            for w in widths
        ],
        out_shape=[
            jax.ShapeDtypeStruct((slots * replicas, rows // replicas, w), jnp.bfloat16)
            for w in widths
        ],
        compiler_params=pltpu.CompilerParams(vmem_limit_bytes=32 * 2**20),
    )(*in_hbm(order, queries, out_grad))


def fill_bias(lengths_ref, bias_ref):
    block_rows = bias_ref.shape[0]
    margin = SPAN * block_rows
    docs = lengths_ref.shape[1]
    lengths = lengths_ref[...].astype(jnp.float32)
    down = lax.broadcasted_iota(jnp.int32, (docs, docs), 0)
    across = lax.broadcasted_iota(jnp.int32, (docs, docs), 1)
    column = jnp.sum(jnp.where(down == across, lengths, 0.0), axis=1, keepdims=True)
    starts = jnp.sum(jnp.where(down < across, column, 0.0), axis=0, keepdims=True)
    first = lax.axis_index("ctx") * block_rows
    place = first + lax.broadcasted_iota(jnp.int32, (block_rows, docs), 0)
    begun = starts <= place.astype(jnp.float32)
    begin = jnp.max(jnp.where(begun, starts, 0.0), axis=1, keepdims=True).astype(jnp.int32)
    begin = begin - (first - margin)
    for t in range(block_rows // TILE):
        here = slice(t * TILE, (t + 1) * TILE)
        row = lax.broadcasted_iota(jnp.int32, (TILE, margin + TILE), 0)
        col = lax.broadcasted_iota(jnp.int32, (TILE, margin + TILE), 1)
        allowed = (col <= row + margin) & (col >= begin[here] - t * TILE)
        bias_ref[here, :] = jnp.where(allowed, 0.0, -1e30)


def stacked(ref, here, begin, heads):
    return jnp.concatenate(
        [ref[here, begin + h * HD : begin + (h + 1) * HD] for h in range(heads)], axis=0
    )


def heads_pass(
    heads, column, rows_ref, key_win, value_win, bias_ref, dk_ref, dv_ref,
    out_stage, dq_stage, out_hbm, dq_hbm, sems,
):
    block_rows = rows_ref.shape[0]
    margin = SPAN * block_rows
    width = margin + TILE
    copies = []
    for t in range(block_rows // TILE):
        here = slice(t * TILE, (t + 1) * TILE)
        window = slice(t * TILE, t * TILE + width)
        query = stacked(rows_ref, here, 0, heads)
        grad = stacked(rows_ref, here, heads * HD, heads)
        key, value = key_win[window, :], value_win[window, :]
        scores = (dot(query, key, NT) * LOG2_SCALE).reshape(heads, TILE, width)
        scores = (scores + bias_ref[here, :][None]).reshape(heads * TILE, width)
        top = jnp.max(scores, axis=1, keepdims=True)
        expo = jnp.exp2(scores - top)
        inverse = 1.0 / jnp.sum(expo, axis=1, keepdims=True)
        prob = expo.astype(jnp.bfloat16)
        output = (dot(prob, value, NN) * inverse).astype(jnp.bfloat16)
        grad = (grad.astype(jnp.float32) * inverse).astype(jnp.bfloat16)
        delta = jnp.sum(
            grad.astype(jnp.float32) * output.astype(jnp.float32), axis=1, keepdims=True
        )
        dprob = dot(grad, value, NT)
        dscore = (prob.astype(jnp.float32) * (dprob - delta)).astype(jnp.bfloat16)
        dquery = (dot(dscore, key, NN) * SCALE).astype(jnp.bfloat16)
        for h in range(heads):
            cols = slice(h * HD, (h + 1) * HD)
            out_stage[here, cols] = output[h * TILE : (h + 1) * TILE]
            dq_stage[here, cols] = dquery[h * TILE : (h + 1) * TILE]
        for which, (stage, target) in enumerate(((out_stage, out_hbm), (dq_stage, dq_hbm))):
            copies.append(
                pltpu.make_async_copy(
                    stage.at[here, :],
                    target.at[here, column * HD : (column + heads) * HD],
                    sems.at[2 * t + which],
                )
            )
            copies[-1].start()
        dv_ref[:, window] += dot(grad, prob, TN)
        dk_ref[:, window] += dot(query, dscore, TN)
    return copies


def gather_window(kv_ref, kv1_ref, kv2_ref, key_win, value_win):
    block_rows = kv_ref.shape[0]
    for place, ref in ((0, kv2_ref), (1, kv1_ref), (2, kv_ref)):
        here = slice(place * block_rows, (place + 1) * block_rows)
        key_win[here, :] = ref[:, :HD]
        value_win[here, :] = ref[:, HD:]


def first_kernel(
    heads, lengths_ref, rows_ref, kv_ref, kv1_ref, kv2_ref,
    out_hbm, dq_hbm, dk_ref, dv_ref,
    key_win, value_win, bias_ref, out_stage, dq_stage, sems,
):
    gather_window(kv_ref, kv1_ref, kv2_ref, key_win, value_win)
    fill_bias(lengths_ref, bias_ref)
    dk_ref[...] = jnp.zeros_like(dk_ref)
    dv_ref[...] = jnp.zeros_like(dv_ref)
    copies = heads_pass(
        heads, 0, rows_ref, key_win, value_win, bias_ref, dk_ref, dv_ref,
        out_stage, dq_stage, out_hbm, dq_hbm, sems,
    )
    for copy in copies:
        copy.wait()


def second_kernel(
    heads, column, lengths_ref, rows_ref, kv_ref, kv1_ref, kv2_ref, dk_in, dv_in, out_in, dq_in,
    out_hbm, dq_hbm, own_ref, back1_ref, back2_ref,
    key_win, value_win, bias_ref, out_stage, dq_stage, sems, dk_ref, dv_ref,
):
    gather_window(kv_ref, kv1_ref, kv2_ref, key_win, value_win)
    fill_bias(lengths_ref, bias_ref)
    dk_ref[...] = dk_in[...]
    dv_ref[...] = dv_in[...]
    copies = heads_pass(
        heads, column, rows_ref, key_win, value_win, bias_ref, dk_ref, dv_ref,
        out_stage, dq_stage, out_hbm, dq_hbm, sems,
    )
    block_rows = rows_ref.shape[0]
    for place, ref in ((0, back2_ref), (1, back1_ref), (2, own_ref)):
        here = slice(place * block_rows, (place + 1) * block_rows)
        ref[:, :HD] = (dk_ref[:, here] * SCALE).T.astype(ref.dtype)
        ref[:, HD:] = dv_ref[:, here].T.astype(ref.dtype)
    for copy in copies:
        copy.wait()


def attend(one, two, key_value, back1, back2, lengths, heads, first):
    block_rows = one.shape[0]
    width = (SPAN + 1) * block_rows
    whole = lambda shape: pl.BlockSpec(shape, lambda: (0, 0))
    anywhere = pl.BlockSpec(memory_space=pl.ANY)
    pair = key_value.shape
    out = pltpu.HBM((block_rows, heads * HD), jnp.bfloat16)
    total = (HD, width)
    params = pltpu.CompilerParams(vmem_limit_bytes=44 * 2**20)
    inputs = [whole(a.shape) for a in (lengths, one, key_value, back1, back2)]

    def scratch(count):
        return [
            pltpu.VMEM((width, HD), jnp.bfloat16),
            pltpu.VMEM((width, HD), jnp.bfloat16),
            pltpu.VMEM((block_rows, SPAN * block_rows + TILE), jnp.float32),
            pltpu.VMEM((block_rows, count * HD), jnp.bfloat16),
            pltpu.VMEM((block_rows, count * HD), jnp.bfloat16),
            pltpu.SemaphoreType.DMA((2 * block_rows // TILE,)),
        ]

    attended, query_grad, dk, dv = pl.pallas_call(
        functools.partial(first_kernel, first),
        in_specs=inputs,
        out_specs=[anywhere, anywhere, whole(total), whole(total)],
        out_shape=[out, out, pltpu.HBM(total, jnp.float32), pltpu.HBM(total, jnp.float32)],
        scratch_shapes=scratch(first),
        compiler_params=params,
    )(lengths, one, key_value, back1, back2)
    inputs[1] = whole(two.shape)
    return pl.pallas_call(
        functools.partial(second_kernel, heads - first, first),
        in_specs=inputs + [whole(total), whole(total), anywhere, anywhere],
        out_specs=[anywhere, anywhere, whole(pair), whole(pair), whole(pair)],
        out_shape=[
            out, out,
            jax.ShapeDtypeStruct(pair, jnp.float32),
            jax.ShapeDtypeStruct(pair, jnp.bfloat16),
            jax.ShapeDtypeStruct(pair, jnp.bfloat16),
        ],
        scratch_shapes=scratch(heads - first)
        + [pltpu.VMEM(total, jnp.float32), pltpu.VMEM(total, jnp.float32)],
        input_output_aliases={7: 0, 8: 1},
        compiler_params=params,
    )(lengths, two, key_value, back1, back2, *in_hbm(dk, dv), attended, query_grad)


def shifted(block, axis, distance):
    devices = range(lax.axis_size(axis))
    route = [(i - distance, i) for i in devices if i - distance in devices]
    return lax.ppermute(block, axis, route)


def exchange(block):
    moved = lax.all_to_all(block, ("tp", "dp"), split_axis=0, concat_axis=0, tiled=True)
    return moved.reshape(moved.shape[0] * moved.shape[1], moved.shape[2])


def on_device(queries, key_rows, values_in, out_grad, send_rows, doc_lengths):
    replicas, slots = lax.axis_size("dp"), lax.axis_size("tp")
    heads = queries.shape[2] // slots // HD
    key_value = pack_small(send_rows[0], key_rows[0], values_in[0], replicas, slots)
    one, two = pack_large(send_rows[0], queries[0], out_grad[0], replicas, slots, FIRST_HEADS)
    key_value = exchange(key_value)
    previous = [shifted(key_value, "ctx", offset) for offset in range(1, SPAN + 1)]
    one = exchange(one)
    one, two, previous = lax.optimization_barrier((one, two, previous))
    two = exchange(two)
    attended, query_grad, own, back1, back2 = attend(
        one, two, key_value, previous[0], previous[1], doc_lengths, heads, FIRST_HEADS
    )
    for offset, part in ((2, back2), (1, back1)):
        own = own + shifted(part, "ctx", -offset).astype(jnp.float32)
    own = own.astype(jnp.bfloat16)
    return (attended[None], query_grad[None], own[None, :, :HD], own[None, :, HD:])


def solution(mesh):
    rows = P("dp", ("ctx", "tp"), None)
    out = P("dp", "ctx", "tp")
    return jax.shard_map(
        on_device,
        mesh=mesh,
        in_specs=(rows, rows, rows, rows, rows, P("dp", None)),
        out_specs=(out, out, out, out),
        check_vma=False,
    )
```

time: 102 us -> 88.4 us (0.87)
  blocking collectives: 23.8 us -> 0 us
  starting transfers between devices: 17.1 us -> 28.6 us
  local copies, waits for them, and re-layouts: 9.72 us -> 1.63 us
  waiting for transfers between devices: 23.2 us -> 27.6 us
  Pallas kernels: 27.3 us -> 29.3 us
    all_to_all x1 -> x0, blocking collectives: 23.8 us -> none  [exchange(): lax.all_to_all(block, ('tp', 'dp'), split_axis=0, concat_axis=0, tiled=True)]
    all_to_all x1 -> x3, starting transfers between devices: 4.33 us -> 15.9 us  [exchange(): lax.all_to_all(block, ('tp', 'dp'), split_axis=0, concat_axis=0, tiled=True)]
    unnamed x20 -> x4, local copies, waits for them, and re-layouts: 8.98 us -> 0.91 us
    ppermute x4, waiting for transfers between devices: 23.2 us -> 26 us  [shifted(): return lax.ppermute(block, axis, route)]
    pallas_call x3 -> x4, Pallas kernels: 27.3 us -> 29.3 us  [the longest x1 13.5 us: attend(): pl.pallas_call(functools.partial(first_kernel, first), in_specs=inputs, o...]
    all_to_all x1 -> x3, waiting for transfers between devices: 0.01 us -> 1.64 us  [exchange(): lax.all_to_all(block, ('tp', 'dp'), split_axis=0, concat_axis=0, tiled=True)]
  transfers between devices with their start and end apart: 5 -> 7, of which waited for: 4 -> 5; matrix products, arithmetic and copies ran while one was open for 0% -> 0% of each run, Pallas kernels for 11% -> 20%
where the time goes in v2:
time: 88.4 us; the launch traced here: 87.9 us
  Pallas kernels  29.3 us (33%)
  starting transfers between devices  28.6 us (32%)
  waiting for transfers between devices  27.6 us (31%)
  local copies, waits for them, and re-layouts  1.63 us (2%)
    ppermute x4, waiting for transfers between devices, shifted(): return lax.ppermute(block, axis, route)  26 us
    all_to_all x3, starting transfers between devices, exchange(): lax.all_to_all(block, ('tp', 'dp'), split_axis=0, concat_axis=0, tiled=True)  15.9 us
    pallas_call x1, Pallas kernels, attend(): pl.pallas_call(functools.partial(first_kernel, first), in_specs=inputs, o...  13.5 us
    ppermute x4, starting transfers between devices, shifted(): return lax.ppermute(block, axis, route)  12.7 us
    pallas_call x1, Pallas kernels, attend(): pl.pallas_call(functools.partial(second_kernel, heads - first, first), in...  9.57 us
    pallas_call x1, Pallas kernels, pack_large(): pl.pallas_call(functools.partial(pack_large_kernel, heads, first), grid=(...  4.26 us
    pallas_call x1, Pallas kernels, pack_small(): pl.pallas_call(pack_small_kernel, in_specs=[whole(order.shape), whole(key...  1.94 us
  transfers between devices with their start and end apart: 7, of which 5 were waited for; matrix products, arithmetic and copies ran while one was open for 0% of the time, Pallas kernels for 20%

profile of v2, /device:TPU:102, one launch (start us, length us, event | category | flops | bytes accessed | tf_op | source)
XLA Modules:
  0.0 87.9 jit_solution(7796283362889739867)
XLA Ops:
  0.6 1.9 %shard_map.94 = bf16[16,32,256]{2,1,0:T(8,128)(2,1)} custom-call(s32[1,64]{1,0:T(1,128)} %bitcast.26, bf16[64,1024]{1,0:T(8,128)(2,1)} %bitcast.24, bf16[64,1024]{1,0:T(8,128)(2,1)} %bitcast.25), custom_call_target="tpu_custom_call" | custom-call | tf_op jit(solution)/shard_map/pallas_call | solution.py:69
  2.6 5.9 %all-to-all-start.1 = ((bf16[16,32,256]{2,1,0:T(8,128)(2,1)}), bf16[16,32,256]{2,1,0:T(8,128)(2,1)S(1)}, u32[]{:S(2)}, u32[]{:S(2)}) async-start(bf16[16,32,256]{2,1,0:T(8,128)(2,1)} %shard_map.94), calls=%async_computation.1 | async-start | bytes 524288 | tf_op jit(solution)/shard_map/all_to_all | solution.py:274
  8.5 4.3 %shard_map.93 = (bf16[16,32,1280]{2,1,0:T(8,128)(2,1)}, bf16[16,32,768]{2,1,0:T(8,128)(2,1)S(1)}) custom-call(s32[1,64]{1,0:T(1,128)} %bitcast.27, bf16[64,8192]{1,0:T(8,128)(2,1)} %bitcast.20, bf16[64,8192]{1,0:T(8,128)(2,1)} %bitcast.21), custom_call_target="tpu_custom_call" | custom-call | tf_op jit(solution)/shard_map/pallas_call | solution.py:83
  12.8 0.0 copy-start
  12.8 0.9 %copy-done = bf16[16,32,768]{2,1,0:T(8,128)(2,1)} copy-done((bf16[16,32,768]{2,1,0:T(8,128)(2,1)}, bf16[16,32,768]{2,1,0:T(8,128)(2,1)S(1)}, u32[]{:S(2)}) %copy-start) | copy-done | bytes 786456
  13.7 1.6 %all-to-all-done.1 = bf16[16,32,256]{2,1,0:T(8,128)(2,1)S(1)} async-done(((bf16[16,32,256]{2,1,0:T(8,128)(2,1)}), bf16[16,32,256]{2,1,0:T(8,128)(2,1)S(1)}, u32[]{:S(2)}, u32[]{:S(2)}) %all-to-all-start.1) | async-done | bytes 262176 | tf_op jit(solution)/shard_map/all_to_all | solution.py:274
  15.3 4.2 %all-to-all-start = ((bf16[16,32,1280]{2,1,0:T(8,128)(2,1)}), bf16[16,32,1280]{2,1,0:T(8,128)(2,1)S(1)}, u32[]{:S(2)}, u32[]{:S(2)}) async-start(bf16[16,32,1280]{2,1,0:T(8,128)(2,1)} %get-tuple-element.19), calls=%async_computation | async-start | bytes 2621440 | tf_op jit(solution)/shard_map/all_to_all | solution.py:274
  19.5 0.0 copy-start.1
  19.5 5.0 %collective-permute-start.1 = (bf16[512,256]{1,0:T(8,128)(2,1)S(1)}, bf16[512,256]{1,0:T(8,128)(2,1)S(1)}, u32[]{:S(2)}, u32[]{:S(2)}) collective-permute-start(bf16[512,256]{1,0:T(8,128)(2,1)S(1)} %bitcast.16), channel_id=1, source_target_pairs={{0,16},{8,24},{16,32},{24,40},{32,48},{40,56},{48,64},{56,72},{64,... | collective-permute-start | bytes 786440 | tf_op jit(solution)/shard_map/ppermute | solution.py:270
  24.6 3.8 %collective-permute-start = (bf16[512,256]{1,0:T(8,128)(2,1)S(1)}, bf16[512,256]{1,0:T(8,128)(2,1)S(1)}, u32[]{:S(2)}, u32[]{:S(2)}) collective-permute-start(bf16[512,256]{1,0:T(8,128)(2,1)S(1)} %bitcast.17), channel_id=1, source_target_pairs={{0,8},{8,16},{16,24},{24,32},{32,40},{40,48},{48,56},{56,64},{64,7... | collective-permute-start | bytes 786440 | tf_op jit(solution)/shard_map/ppermute | solution.py:270
  28.3 2.9 %collective-permute-done.1.kv2_ref = bf16[512,256]{1,0:T(8,128)(2,1)S(1)} collective-permute-done((bf16[512,256]{1,0:T(8,128)(2,1)S(1)}, bf16[512,256]{1,0:T(8,128)(2,1)S(1)}, u32[]{:S(2)}, u32[]{:S(2)}) %collective-permute-start.1) | collective-permute-done | bytes 262176 | tf_op jit(solution)/shard_map/ppermute | solution.py:270
  31.2 10.8 %collective-permute-done.kv1_ref = bf16[512,256]{1,0:T(8,128)(2,1)S(1)} collective-permute-done((bf16[512,256]{1,0:T(8,128)(2,1)S(1)}, bf16[512,256]{1,0:T(8,128)(2,1)S(1)}, u32[]{:S(2)}, u32[]{:S(2)}) %collective-permute-start) | collective-permute-done | bytes 262176 | tf_op jit(solution)/shard_map/ppermute | solution.py:270
  42.0 0.0 all-to-all-done
  42.0 5.7 %all-to-all-start.2 = ((bf16[16,32,768]{2,1,0:T(8,128)(2,1)}), bf16[16,32,768]{2,1,0:T(8,128)(2,1)S(1)}, u32[]{:S(2)}, u32[]{:S(2)}) async-start(bf16[16,32,768]{2,1,0:T(8,128)(2,1)} %copy-done), calls=%async_computation.2 | async-start | bytes 1572864 | tf_op jit(solution)/shard_map/all_to_all | solution.py:274
  47.8 0.0 copy-done.1
  47.8 13.5 %shard_map.95 = (bf16[512,1024]{1,0:T(8,128)(2,1)}, bf16[512,1024]{1,0:T(8,128)(2,1)}, f32[128,1536]{1,0:T(8,128)}, f32[128,1536]{1,0:T(8,128)}) custom-call(s32[1,32]{1,0:T(1,128)S(1)} %copy-done.1, bf16[512,1280]{1,0:T(8,128)(2,1)S(1)} %bitcast.14, bf16[512,256]{1,0:T(8,128)(2,1)S(1)} %bitcast.18, bf16[512,256]{1,0:T(8,128)(2,1)S(1)} %collective-permute-done.kv1_ref, ...), custom_call_target="tpu_custom_call" | custom-call | tf_op jit(solution)/shard_map/pallas_call | solution.py:241
  61.3 0.0 all-to-all-done.2
  61.3 9.6 %shard_map.96 = (bf16[512,1024]{1,0:T(8,128)(2,1)}, bf16[512,1024]{1,0:T(8,128)(2,1)}, f32[512,256]{1,0:T(8,128)S(1)}, bf16[512,256]{1,0:T(8,128)(2,1)S(1)}, bf16[512,256]{1,0:T(8,128)(2,1)S(1)}) custom-call(s32[1,32]{1,0:T(1,128)S(1)} %copy-done.1, bf16[512,768]{1,0:T(8,128)(2,1)S(1)} %bitcast.15, ...), custom_call_target="tpu_custom_call", output_to_operand_aliasing={{0}: (7, {}), {1}: (8, {})} | custom-call | tf_op jit(solution)/shard_map/pallas_call | solution.py:250
  70.8 2.0 %collective-permute-start.2 = (bf16[512,256]{1,0:T(8,128)(2,1)S(1)}, bf16[512,256]{1,0:T(8,128)(2,1)S(1)}, u32[]{:S(2)}, u32[]{:S(2)}) collective-permute-start(bf16[512,256]{1,0:T(8,128)(2,1)S(1)} %get-tuple-element.32), channel_id=1, source_target_pairs={{16,0},{24,8},{32,16},{40,24},{48,32},{56,40},{64,48},{72,56},{80,... | collective-permute-start | bytes 786440 | tf_op jit(solution)/shard_map/ppermute | solution.py:270
  72.9 1.9 %collective-permute-start.3 = (bf16[512,256]{1,0:T(8,128)(2,1)S(1)}, bf16[512,256]{1,0:T(8,128)(2,1)S(1)}, u32[]{:S(2)}, u32[]{:S(2)}) collective-permute-start(bf16[512,256]{1,0:T(8,128)(2,1)S(1)} %get-tuple-element.33), channel_id=1, source_target_pairs={{8,0},{16,8},{24,16},{32,24},{40,32},{48,40},{56,48},{64,56},{72,6... | collective-permute-start | bytes 786440 | tf_op jit(solution)/shard_map/ppermute | solution.py:270
  74.8 7.7 %collective-permute-done.2 = bf16[512,256]{1,0:T(8,128)(2,1)S(1)} collective-permute-done((bf16[512,256]{1,0:T(8,128)(2,1)S(1)}, bf16[512,256]{1,0:T(8,128)(2,1)S(1)}, u32[]{:S(2)}, u32[]{:S(2)}) %collective-permute-start.2) | collective-permute-done | bytes 262176 | tf_op jit(solution)/shard_map/ppermute | solution.py:270
  82.5 4.6 %collective-permute-done.3 = bf16[512,256]{1,0:T(8,128)(2,1)S(1)} collective-permute-done((bf16[512,256]{1,0:T(8,128)(2,1)S(1)}, bf16[512,256]{1,0:T(8,128)(2,1)S(1)}, u32[]{:S(2)}, u32[]{:S(2)}) %collective-permute-start.3) | collective-permute-done | bytes 262176 | tf_op jit(solution)/shard_map/ppermute | solution.py:270
  87.1 0.1 add_convert_fusion
  87.2 0.7 slice_bitcast_fusion
Async XLA Ops:
  2.6 12.7 %all-to-all-start.1 = ((bf16[16,32,256]{2,1,0:T(8,128)(2,1)}), bf16[16,32,256]{2,1,0:T(8,128)(2,1)S(1)}, u32[]{:S(2)}, u32[]{:S(2)}) async-start(bf16[16,32,256]{2,1,0:T(8,128)(2,1)} %shard_map.94), calls=%async_computation.1 | async-start | bytes 524288 | tf_op jit(solution)/shard_map/all_to_all | solution.py:274
  12.8 0.9 %copy-start = (bf16[16,32,768]{2,1,0:T(8,128)(2,1)}, bf16[16,32,768]{2,1,0:T(8,128)(2,1)S(1)}, u32[]{:S(2)}) copy-start(bf16[16,32,768]{2,1,0:T(8,128)(2,1)S(1)} %get-tuple-element.21) | copy-start | bytes 2359300
  15.3 26.7 %all-to-all-start = ((bf16[16,32,1280]{2,1,0:T(8,128)(2,1)}), bf16[16,32,1280]{2,1,0:T(8,128)(2,1)S(1)}, u32[]{:S(2)}, u32[]{:S(2)}) async-start(bf16[16,32,1280]{2,1,0:T(8,128)(2,1)} %get-tuple-element.19), calls=%async_computation | async-start | bytes 2621440 | tf_op jit(solution)/shard_map/all_to_all | solution.py:274
  19.5 28.2 %copy-start.1 = (s32[1,32]{1,0:T(1,128)S(1)}, s32[1,32]{1,0:T(1,128)}, u32[]{:S(2)}) copy-start(s32[1,32]{1,0:T(1,128)} %lengths_ref.3) | copy-start | bytes 388
  19.5 11.7 %collective-permute-start.1 = (bf16[512,256]{1,0:T(8,128)(2,1)S(1)}, bf16[512,256]{1,0:T(8,128)(2,1)S(1)}, u32[]{:S(2)}, u32[]{:S(2)}) collective-permute-start(bf16[512,256]{1,0:T(8,128)(2,1)S(1)} %bitcast.16), channel_id=1, source_target_pairs={{0,16},{8,24},{16,32},{24,40},{32,48},{40,56},{48,64},{56,72},{64,... | collective-permute-start | bytes 786440 | tf_op jit(solution)/shard_map/ppermute | solution.py:270
  24.6 17.4 %collective-permute-start = (bf16[512,256]{1,0:T(8,128)(2,1)S(1)}, bf16[512,256]{1,0:T(8,128)(2,1)S(1)}, u32[]{:S(2)}, u32[]{:S(2)}) collective-permute-start(bf16[512,256]{1,0:T(8,128)(2,1)S(1)} %bitcast.17), channel_id=1, source_target_pairs={{0,8},{8,16},{16,24},{24,32},{32,40},{40,48},{48,56},{56,64},{64,7... | collective-permute-start | bytes 786440 | tf_op jit(solution)/shard_map/ppermute | solution.py:270
  42.0 19.2 %all-to-all-start.2 = ((bf16[16,32,768]{2,1,0:T(8,128)(2,1)}), bf16[16,32,768]{2,1,0:T(8,128)(2,1)S(1)}, u32[]{:S(2)}, u32[]{:S(2)}) async-start(bf16[16,32,768]{2,1,0:T(8,128)(2,1)} %copy-done), calls=%async_computation.2 | async-start | bytes 1572864 | tf_op jit(solution)/shard_map/all_to_all | solution.py:274
  70.8 11.7 %collective-permute-start.2 = (bf16[512,256]{1,0:T(8,128)(2,1)S(1)}, bf16[512,256]{1,0:T(8,128)(2,1)S(1)}, u32[]{:S(2)}, u32[]{:S(2)}) collective-permute-start(bf16[512,256]{1,0:T(8,128)(2,1)S(1)} %get-tuple-element.32), channel_id=1, source_target_pairs={{16,0},{24,8},{32,16},{40,24},{48,32},{56,40},{64,48},{72,56},{80,... | collective-permute-start | bytes 786440 | tf_op jit(solution)/shard_map/ppermute | solution.py:270
  72.9 14.2 %collective-permute-start.3 = (bf16[512,256]{1,0:T(8,128)(2,1)S(1)}, bf16[512,256]{1,0:T(8,128)(2,1)S(1)}, u32[]{:S(2)}, u32[]{:S(2)}) collective-permute-start(bf16[512,256]{1,0:T(8,128)(2,1)S(1)} %get-tuple-element.33), channel_id=1, source_target_pairs={{8,0},{16,8},{24,16},{32,24},{40,32},{48,40},{56,48},{64,56},{72,6... | collective-permute-start | bytes 786440 | tf_op jit(solution)/shard_map/ppermute | solution.py:270

commit v3 on v2

v3 whole, which is shorter than its diff:
```python
import functools
import math

import jax
import jax.numpy as jnp
from jax import lax
from jax.experimental import pallas as pl
from jax.experimental.pallas import tpu as pltpu
from jax.sharding import PartitionSpec as P

HD = 128
SPAN = 2
FRONT_HEADS = 4
BACK_HEADS = 4
PACK_SLOTS = 2
TILE = 256
SCALE = 1.0 / math.sqrt(HD)
LOG2_SCALE = math.log2(math.e) * SCALE
NT = (((1,), (1,)), ((), ()))
NN = (((1,), (0,)), ((), ()))
TN = (((0,), (0,)), ((), ()))


def dot(a, b, dims):
    return lax.dot_general(a, b, dims, preferred_element_type=jnp.float32)


def select(order_ref):
    rows = order_ref.shape[1]
    row = lax.broadcasted_iota(jnp.int32, (rows, rows), 0)
    return (row == order_ref[...]).astype(jnp.bfloat16)


def put(ref, slot, begin, moved):
    group = ref.shape[1]
    replicas = moved.shape[0] // group
    for replica in range(replicas):
        ref[slot * replicas + replica, :, begin : begin + moved.shape[1]] = moved[
            replica * group : (replica + 1) * group
        ]


def pack_small_kernel(order_ref, k_ref, v_ref, sent_ref):
    pick = select(order_ref)
    for begin, ref in ((0, k_ref), (HD, v_ref)):
        moved = dot(pick, ref[...], TN).astype(jnp.bfloat16)
        for slot in range(moved.shape[1] // HD):
            put(sent_ref, slot, begin, moved[:, slot * HD : (slot + 1) * HD])


def pack_large_kernel(order_ref, q_ref, g_ref, sent_ref):
    pick = select(order_ref)
    half = sent_ref.shape[2] // 2
    for index, ref in enumerate((q_ref, g_ref)):
        for slot in range(ref.shape[1] // half):
            moved = dot(pick, ref[:, slot * half : (slot + 1) * half], TN)
            put(sent_ref, slot, index * half, moved.astype(jnp.bfloat16))


def in_hbm(*arrays):
    return [pltpu.with_memory_space_constraint(a, pltpu.HBM) for a in arrays]


def pack_small(order, key_rows, values_in, replicas, slots):
    rows, columns = key_rows.shape
    whole = lambda shape: pl.BlockSpec(shape, lambda: (0,) * len(shape))
    sent = (slots * replicas, rows // replicas, 2 * columns // slots)
    return pl.pallas_call(
        pack_small_kernel,
        in_specs=[whole(order.shape), whole(key_rows.shape), whole(values_in.shape)],
        out_specs=whole(sent),
        out_shape=jax.ShapeDtypeStruct(sent, jnp.bfloat16),
        compiler_params=pltpu.CompilerParams(vmem_limit_bytes=16 * 2**20),
    )(*in_hbm(order, key_rows, values_in))


def pack_large(order, queries, out_grad, replicas, slots):
    rows, columns = queries.shape
    half = columns // slots
    wide = pl.BlockSpec((rows, PACK_SLOTS * half), lambda t: (0, t))
    sent = (slots * replicas, rows // replicas, 2 * half)
    return pl.pallas_call(
        pack_large_kernel,
        grid=(slots // PACK_SLOTS,),
        in_specs=[pl.BlockSpec(order.shape, lambda t: (0, 0)), wide, wide],
        out_specs=pl.BlockSpec((PACK_SLOTS * replicas,) + sent[1:], lambda t: (t, 0, 0)),
        out_shape=jax.ShapeDtypeStruct(sent, jnp.bfloat16),
        compiler_params=pltpu.CompilerParams(vmem_limit_bytes=32 * 2**20),
    )(*in_hbm(order, queries, out_grad))


def begin_kernel(lengths_ref, begin_ref):
    block_rows = begin_ref.shape[0]
    docs = lengths_ref.shape[1]
    lengths = lengths_ref[...].astype(jnp.float32)
    down = lax.broadcasted_iota(jnp.int32, (docs, docs), 0)
    across = lax.broadcasted_iota(jnp.int32, (docs, docs), 1)
    column = jnp.sum(jnp.where(down == across, lengths, 0.0), axis=1, keepdims=True)
    starts = jnp.sum(jnp.where(down < across, column, 0.0), axis=0, keepdims=True)
    first = lax.axis_index("ctx") * block_rows
    place = first + lax.broadcasted_iota(jnp.int32, (block_rows, docs), 0)
    begun = starts <= place.astype(jnp.float32)
    begin = jnp.max(jnp.where(begun, starts, 0.0), axis=1, keepdims=True).astype(jnp.int32)
    begin_ref[...] = jnp.broadcast_to(begin - (first - SPAN * block_rows), begin_ref.shape)


def mask(begin, margin, width):
    rows = begin.shape[0]
    row = lax.broadcasted_iota(jnp.int32, (rows, width), 0)
    col = lax.broadcasted_iota(jnp.int32, (rows, width), 1)
    return jnp.where((col <= row + margin) & (col >= begin), 0.0, -1e30)


def stacked(ref, here, begin, heads):
    return jnp.concatenate(
        [ref[here, begin + h * HD : begin + (h + 1) * HD] for h in range(heads)], axis=0
    )


def gather_window(kv_ref, kv1_ref, kv2_ref, key_win, value_win):
    block_rows = kv_ref.shape[0]
    for place, ref in ((0, kv2_ref), (1, kv1_ref), (2, kv_ref)):
        here = slice(place * block_rows, (place + 1) * block_rows)
        key_win[here, :] = ref[:, :HD]
        value_win[here, :HD] = ref[:, HD:]


def front_kernel(
    heads, begin_ref, rows_ref, kv_ref, kv1_ref, kv2_ref,
    prob_ref, dscore_ref, back1_ref, back2_ref,
    key_win, value_win, dk_ref, dv_ref, bias_ref,
):
    gather_window(kv_ref, kv1_ref, kv2_ref, key_win, value_win)
    dk_ref[...] = jnp.zeros_like(dk_ref)
    dv_ref[...] = jnp.zeros_like(dv_ref)
    block_rows = rows_ref.shape[0]
    margin = SPAN * block_rows
    width = margin + TILE
    for head in range(0, heads, FRONT_HEADS):
        for t in range(block_rows // TILE):
            here = slice(t * TILE, (t + 1) * TILE)
            window = slice(t * TILE, t * TILE + width)
            query = stacked(rows_ref, here, head * HD, FRONT_HEADS)
            grad = stacked(rows_ref, here, (heads + head) * HD, FRONT_HEADS)
            scores = dot(query, key_win[window, :], NT)
            if head == 0:
                bias_ref[here, :] = mask(begin_ref[here, :1] - t * TILE, margin, width)
            scores = (scores * LOG2_SCALE).reshape(FRONT_HEADS, TILE, width)
            scores = (scores + bias_ref[here, :][None]).reshape(FRONT_HEADS * TILE, width)
            top = jnp.max(scores, axis=1, keepdims=True)
            expo = jnp.exp2(scores - top)
            inverse = 1.0 / jnp.sum(expo, axis=1, keepdims=True)
            prob = expo.astype(jnp.bfloat16)
            dprob = dot(grad, value_win[window, :], NT)
            delta = jnp.sum(expo * dprob, axis=1, keepdims=True) * inverse
            dscore = (expo * (dprob - delta)).astype(jnp.bfloat16)
            query = (query.astype(jnp.float32) * inverse).astype(jnp.bfloat16)
            grad = (grad.astype(jnp.float32) * inverse).astype(jnp.bfloat16)
            for h in range(FRONT_HEADS):
                part = slice(h * TILE, (h + 1) * TILE)
                prob_ref[head + h, here, :] = prob[part]
                dscore_ref[head + h, here, :] = dscore[part]
            before = margin - t * TILE
            past = slice(t * TILE, margin)
            dv_ref[:, past] += dot(grad, prob[:, :before], TN)
            dk_ref[:, past] += dot(query, dscore[:, :before], TN)
    for place, ref in ((0, back2_ref), (1, back1_ref)):
        here = slice(place * block_rows, (place + 1) * block_rows)
        ref[:, :HD] = (dk_ref[:, here] * SCALE).T.astype(ref.dtype)
        ref[:, HD:] = dv_ref[:, here].T.astype(ref.dtype)


def back_kernel(
    heads, rows_ref, kv_ref, kv1_ref, kv2_ref, prob_ref, dscore_ref,
    out_ref, dq_ref, own_ref,
    key_win, value_win, dk_ref, dv_ref,
):
    gather_window(kv_ref, kv1_ref, kv2_ref, key_win, value_win)
    value_win[:, HD:] = jnp.ones_like(value_win[:, HD:])
    dk_ref[...] = jnp.zeros_like(dk_ref)
    dv_ref[...] = jnp.zeros_like(dv_ref)
    block_rows = rows_ref.shape[0]
    margin = SPAN * block_rows
    width = margin + TILE
    for head in range(0, heads, BACK_HEADS):
        for t in range(block_rows // TILE):
            here = slice(t * TILE, (t + 1) * TILE)
            window = slice(t * TILE, t * TILE + width)
            group = lambda ref: jnp.concatenate(
                [ref[head + h, here, :] for h in range(BACK_HEADS)], axis=0
            )
            prob, dscore = group(prob_ref), group(dscore_ref)
            both = dot(prob, value_win[window, :], NN)
            inverse = 1.0 / both[:, HD:]
            output = (both[:, :HD] * inverse).astype(jnp.bfloat16)
            dquery = dot(dscore, key_win[window, :], NN) * (inverse * SCALE)
            dquery = dquery.astype(jnp.bfloat16)
            for h in range(BACK_HEADS):
                cols = slice((head + h) * HD, (head + h + 1) * HD)
                out_ref[here, cols] = output[h * TILE : (h + 1) * TILE]
                dq_ref[here, cols] = dquery[h * TILE : (h + 1) * TILE]
            query = stacked(rows_ref, here, head * HD, BACK_HEADS)
            grad = stacked(rows_ref, here, (heads + head) * HD, BACK_HEADS)
            query = (query.astype(jnp.float32) * inverse).astype(jnp.bfloat16)
            grad = (grad.astype(jnp.float32) * inverse).astype(jnp.bfloat16)
            before = margin - t * TILE
            reach = slice(0, (t + 1) * TILE)
            dv_ref[:, reach] += dot(grad, prob[:, before:], TN)
            dk_ref[:, reach] += dot(query, dscore[:, before:], TN)
    own_ref[:, :HD] = (dk_ref[...] * SCALE).T
    own_ref[:, HD:] = dv_ref[...].T


def attend(rows, key_value, kv1, kv2, begin, heads):
    block_rows = rows.shape[0]
    margin = SPAN * block_rows
    width = margin + TILE
    pair = key_value.shape
    vmem = pl.BlockSpec(memory_space=pltpu.VMEM)
    whole = lambda shape: pl.BlockSpec(shape, lambda: (0,) * len(shape))
    out = jax.ShapeDtypeStruct((block_rows, heads * HD), jnp.bfloat16)
    sent = jax.ShapeDtypeStruct(pair, jnp.bfloat16)
    work = heads * block_rows * width * HD
    weights = pltpu.VMEM((heads, block_rows, width), jnp.bfloat16)
    inputs = [rows, key_value, kv1, kv2]
    specs = [whole(a.shape) for a in inputs]

    def scratch(value_columns, columns):
        return [
            pltpu.VMEM((margin + block_rows, HD), jnp.bfloat16),
            pltpu.VMEM((margin + block_rows, value_columns), jnp.bfloat16),
            pltpu.VMEM((HD, columns), jnp.float32),
            pltpu.VMEM((HD, columns), jnp.float32),
        ]

    prob, dscore, back1, back2 = pl.pallas_call(
        functools.partial(front_kernel, heads),
        in_specs=[whole(begin.shape)] + specs,
        out_specs=[vmem, vmem, whole(pair), whole(pair)],
        out_shape=[weights, weights, sent, sent],
        scratch_shapes=scratch(HD, margin)
        + [pltpu.VMEM((block_rows, width), jnp.float32)],
        compiler_params=pltpu.CompilerParams(vmem_limit_bytes=25 * 2**20),
        cost_estimate=pl.CostEstimate(
            flops=7 * work, bytes_accessed=8 * work // HD, transcendentals=work // HD
        ),
    )(begin, *inputs)
    attended, query_grad, own = pl.pallas_call(
        functools.partial(back_kernel, heads),
        in_specs=specs + [vmem, vmem],
        out_specs=[whole(out.shape), whole(out.shape), whole(pair)],
        out_shape=[out, out, jax.ShapeDtypeStruct(pair, jnp.float32)],
        scratch_shapes=scratch(2 * HD, block_rows),
        compiler_params=pltpu.CompilerParams(vmem_limit_bytes=18 * 2**20),
        cost_estimate=pl.CostEstimate(
            flops=5 * work, bytes_accessed=8 * work // HD, transcendentals=0
        ),
    )(*inputs, prob, dscore)
    return attended, query_grad, own, back1, back2


def document_begins(lengths, block_rows):
    return pl.pallas_call(
        begin_kernel,
        in_specs=[pl.BlockSpec(lengths.shape, lambda: (0, 0))],
        out_specs=pl.BlockSpec(memory_space=pltpu.VMEM),
        out_shape=pltpu.VMEM((block_rows, HD), jnp.int32),
        compiler_params=pltpu.CompilerParams(vmem_limit_bytes=8 * 2**20),
    )(*in_hbm(lengths))


def shifted(block, axis, distance):
    devices = range(lax.axis_size(axis))
    route = [(i - distance, i) for i in devices if i - distance in devices]
    return lax.ppermute(block, axis, route)


def exchange(block):
    moved = lax.all_to_all(block, ("tp", "dp"), split_axis=0, concat_axis=0, tiled=True)
    return moved.reshape(moved.shape[0] * moved.shape[1], moved.shape[2])


def on_device(queries, key_rows, values_in, out_grad, send_rows, doc_lengths):
    replicas, slots = lax.axis_size("dp"), lax.axis_size("tp")
    heads = queries.shape[2] // slots // HD
    key_value = pack_small(send_rows[0], key_rows[0], values_in[0], replicas, slots)
    rows = pack_large(send_rows[0], queries[0], out_grad[0], replicas, slots)
    key_value = exchange(key_value)
    previous = [shifted(key_value, "ctx", offset) for offset in range(1, SPAN + 1)]
    block_rows = key_value.shape[0]
    lengths, key_value = lax.optimization_barrier((doc_lengths, key_value))
    begin = document_begins(lengths, block_rows)
    rows = exchange(rows)
    attended, query_grad, own, back1, back2 = attend(
        rows, key_value, previous[0], previous[1], begin, heads
    )
    for offset, part in ((2, back2), (1, back1)):
        own = own + shifted(part, "ctx", -offset).astype(jnp.float32)
    own = own.astype(jnp.bfloat16)
    return (attended[None], query_grad[None], own[None, :, :HD], own[None, :, HD:])


def solution(mesh):
    rows = P("dp", ("ctx", "tp"), None)
    out = P("dp", "ctx", "tp")
    return jax.shard_map(
        on_device,
        mesh=mesh,
        in_specs=(rows, rows, rows, rows, rows, P("dp", None)),
        out_specs=(out, out, out, out),
        check_vma=False,
    )
```

time: 88.4 us -> 82 us (0.928)
  starting transfers between devices: 28.6 us -> 22.9 us
  Pallas kernels: 29.3 us -> 27.6 us
    all_to_all x3 -> x2, starting transfers between devices: 15.9 us -> 10.2 us  [exchange(): lax.all_to_all(block, ('tp', 'dp'), split_axis=0, concat_axis=0, tiled=True)]
    pallas_call x3 -> x4, Pallas kernels: 27.3 us -> 25.6 us  [the longest x1 13.8 us: attend(): pl.pallas_call(functools.partial(front_kernel, heads), in_specs=[whole(be...]
    all_to_all x3 -> x2, waiting for transfers between devices: 1.64 us -> 2.33 us  [exchange(): lax.all_to_all(block, ('tp', 'dp'), split_axis=0, concat_axis=0, tiled=True)]
  transfers between devices with their start and end apart: 7 -> 6, of which waited for: 5 -> 4; matrix products, arithmetic and copies ran while one was open for 0% -> 0% of each run, Pallas kernels for 20% -> 15%
where the time goes in v3:
time: 82 us; the launch traced here: 81.6 us
  waiting for transfers between devices  28.3 us (35%)
  Pallas kernels  27.6 us (34%)
  starting transfers between devices  22.9 us (28%)
  local copies, waits for them, and re-layouts  2.04 us (2%)
    ppermute x4, waiting for transfers between devices, shifted(): return lax.ppermute(block, axis, route)  26 us
    pallas_call x1, Pallas kernels, attend(): pl.pallas_call(functools.partial(front_kernel, heads), in_specs=[whole(be...  13.8 us
    ppermute x4, starting transfers between devices, shifted(): return lax.ppermute(block, axis, route)  12.7 us
    all_to_all x2, starting transfers between devices, exchange(): lax.all_to_all(block, ('tp', 'dp'), split_axis=0, concat_axis=0, tiled=True)  10.2 us
    pallas_call x1, Pallas kernels, attend(): pl.pallas_call(functools.partial(back_kernel, heads), in_specs=specs + [v...  7.81 us
    pallas_call x1, Pallas kernels, pack_large(): pl.pallas_call(pack_large_kernel, grid=(slots // PACK_SLOTS,), in_specs=[...  3.14 us
    all_to_all x2, waiting for transfers between devices, exchange(): lax.all_to_all(block, ('tp', 'dp'), split_axis=0, concat_axis=0, tiled=True)  2.33 us
    pallas_call x1, Pallas kernels, pack_small(): pl.pallas_call(pack_small_kernel, in_specs=[whole(order.shape), whole(key...  1.94 us
  transfers between devices with their start and end apart: 6, of which 4 were waited for; matrix products, arithmetic and copies ran while one was open for 0% of the time, Pallas kernels for 15%

profile of v3, /device:TPU:102, one launch (start us, length us, event | category | flops | bytes accessed | tf_op | source)
XLA Modules:
  0.0 81.6 jit_solution(5699042721445758754)
XLA Ops:
  0.6 1.9 %shard_map.94 = bf16[16,32,256]{2,1,0:T(8,128)(2,1)} custom-call(s32[1,64]{1,0:T(1,128)} %bitcast.23, bf16[64,1024]{1,0:T(8,128)(2,1)} %bitcast.21, bf16[64,1024]{1,0:T(8,128)(2,1)} %bitcast.22), custom_call_target="tpu_custom_call" | custom-call | tf_op jit(solution)/shard_map/pallas_call | solution.py:68
  2.6 5.9 %all-to-all-start.1 = ((bf16[16,32,256]{2,1,0:T(8,128)(2,1)}), bf16[16,32,256]{2,1,0:T(8,128)(2,1)S(1)}, u32[]{:S(2)}, u32[]{:S(2)}) async-start(bf16[16,32,256]{2,1,0:T(8,128)(2,1)} %shard_map.94), calls=%async_computation.1 | async-start | bytes 524288 | tf_op jit(solution)/shard_map/all_to_all | solution.py:279
  8.5 3.1 %shard_map.93 = bf16[16,32,2048]{2,1,0:T(8,128)(2,1)S(1)} custom-call(s32[1,64]{1,0:T(1,128)} %bitcast.24, bf16[64,8192]{1,0:T(8,128)(2,1)} %bitcast.19, bf16[64,8192]{1,0:T(8,128)(2,1)} %bitcast.20), custom_call_target="tpu_custom_call" | custom-call | tf_op jit(solution)/shard_map/pallas_call | solution.py:82
  11.7 0.0 copy-start
  11.7 1.3 %copy-done = bf16[16,32,2048]{2,1,0:T(8,128)(2,1)} copy-done((bf16[16,32,2048]{2,1,0:T(8,128)(2,1)}, bf16[16,32,2048]{2,1,0:T(8,128)(2,1)S(1)}, u32[]{:S(2)}) %copy-start) | copy-done | bytes 2097176
  13.0 2.3 %all-to-all-done.1 = bf16[16,32,256]{2,1,0:T(8,128)(2,1)S(1)} async-done(((bf16[16,32,256]{2,1,0:T(8,128)(2,1)}), bf16[16,32,256]{2,1,0:T(8,128)(2,1)S(1)}, u32[]{:S(2)}, u32[]{:S(2)}) %all-to-all-start.1) | async-done | bytes 262176 | tf_op jit(solution)/shard_map/all_to_all | solution.py:279
  15.3 4.2 %all-to-all-start = ((bf16[16,32,2048]{2,1,0:T(8,128)(2,1)}), bf16[16,32,2048]{2,1,0:T(8,128)(2,1)S(1)}, u32[]{:S(2)}, u32[]{:S(2)}) async-start(bf16[16,32,2048]{2,1,0:T(8,128)(2,1)} %copy-done), calls=%async_computation | async-start | bytes 4194304 | tf_op jit(solution)/shard_map/all_to_all | solution.py:279
  19.5 5.0 %collective-permute-start.1 = (bf16[512,256]{1,0:T(8,128)(2,1)S(1)}, bf16[512,256]{1,0:T(8,128)(2,1)S(1)}, u32[]{:S(2)}, u32[]{:S(2)}) collective-permute-start(bf16[512,256]{1,0:T(8,128)(2,1)S(1)} %bitcast.15), channel_id=1, source_target_pairs={{0,16},{8,24},{16,32},{24,40},{32,48},{40,56},{48,64},{56,72},{64,... | collective-permute-start | bytes 786440 | tf_op jit(solution)/shard_map/ppermute | solution.py:275
  24.6 3.8 %collective-permute-start = (bf16[512,256]{1,0:T(8,128)(2,1)S(1)}, bf16[512,256]{1,0:T(8,128)(2,1)S(1)}, u32[]{:S(2)}, u32[]{:S(2)}) collective-permute-start(bf16[512,256]{1,0:T(8,128)(2,1)S(1)} %bitcast.16), channel_id=1, source_target_pairs={{0,8},{8,16},{16,24},{24,32},{32,40},{40,48},{48,56},{56,64},{64,7... | collective-permute-start | bytes 786440 | tf_op jit(solution)/shard_map/ppermute | solution.py:275
  28.3 0.9 %shard_map.95.begin_ref = s32[512,128]{1,0:T(8,128)S(1)} custom-call(s32[1,32]{1,0:T(1,128)} %lengths_ref), custom_call_target="tpu_custom_call" | custom-call | tf_op jit(solution)/shard_map/pallas_call | solution.py:263
  29.2 2.0 %collective-permute-done.1.kv2_ref = bf16[512,256]{1,0:T(8,128)(2,1)S(1)} collective-permute-done((bf16[512,256]{1,0:T(8,128)(2,1)S(1)}, bf16[512,256]{1,0:T(8,128)(2,1)S(1)}, u32[]{:S(2)}, u32[]{:S(2)}) %collective-permute-start.1) | collective-permute-done | bytes 262176 | tf_op jit(solution)/shard_map/ppermute | solution.py:275
  31.2 20.0 %collective-permute-done.kv1_ref = bf16[512,256]{1,0:T(8,128)(2,1)S(1)} collective-permute-done((bf16[512,256]{1,0:T(8,128)(2,1)S(1)}, bf16[512,256]{1,0:T(8,128)(2,1)S(1)}, u32[]{:S(2)}, u32[]{:S(2)}) %collective-permute-start) | collective-permute-done | bytes 262176 | tf_op jit(solution)/shard_map/ppermute | solution.py:275
  51.3 0.0 all-to-all-done
  51.3 13.8 %shard_map.96 = (bf16[8,512,1280]{2,1,0:T(8,128)(2,1)S(1)}, bf16[8,512,1280]{2,1,0:T(8,128)(2,1)S(1)}, bf16[512,256]{1,0:T(8,128)(2,1)S(1)}, bf16[512,256]{1,0:T(8,128)(2,1)S(1)}) custom-call(s32[512,128]{1,0:T(8,128)S(1)} %shard_map.95.begin_ref, bf16[512,2048]{1,0:T(8,128)(2,1)S(1)} %bitcast.13, bf16[512,256]{1,0:T(8,128)(2,1)S(1)} %bitcast.17, ...), custom_call_target="tpu_custom_call" | custom-call | flops 4697620480 | bytes 41943040 | tf_op jit(solution)/shard_map/pallas_call | solution.py:236
  65.0 2.0 %collective-permute-start.2 = (bf16[512,256]{1,0:T(8,128)(2,1)S(1)}, bf16[512,256]{1,0:T(8,128)(2,1)S(1)}, u32[]{:S(2)}, u32[]{:S(2)}) collective-permute-start(bf16[512,256]{1,0:T(8,128)(2,1)S(1)} %get-tuple-element.20), channel_id=1, source_target_pairs={{16,0},{24,8},{32,16},{40,24},{48,32},{56,40},{64,48},{72,56},{80,... | collective-permute-start | bytes 786440 | tf_op jit(solution)/shard_map/ppermute | solution.py:275
  67.1 1.9 %collective-permute-start.3 = (bf16[512,256]{1,0:T(8,128)(2,1)S(1)}, bf16[512,256]{1,0:T(8,128)(2,1)S(1)}, u32[]{:S(2)}, u32[]{:S(2)}) collective-permute-start(bf16[512,256]{1,0:T(8,128)(2,1)S(1)} %get-tuple-element.21), channel_id=1, source_target_pairs={{8,0},{16,8},{24,16},{32,24},{40,32},{48,40},{56,48},{64,56},{72,6... | collective-permute-start | bytes 786440 | tf_op jit(solution)/shard_map/ppermute | solution.py:275
  69.0 7.8 %shard_map.97 = (bf16[512,1024]{1,0:T(8,128)(2,1)}, bf16[512,1024]{1,0:T(8,128)(2,1)}, f32[512,256]{1,0:T(8,128)S(1)}) custom-call(bf16[512,2048]{1,0:T(8,128)(2,1)S(1)} %bitcast.14, bf16[512,256]{1,0:T(8,128)(2,1)S(1)} %bitcast.18, bf16[512,256]{1,0:T(8,128)(2,1)S(1)} %collective-permute-done.kv1_ref, bf16[512,256]{1,0:T(8,128)(2,1)S(1)} %collective-permute-done.1.kv2_ref, ...), custom_call_target="tpu_custom_call" | custom-call | flops 3355443200 | bytes 41943040 | tf_op jit(solution)/shard_map/pallas_call | solution.py:248
  76.8 0.0 collective-permute-done.2
  76.8 4.0 %collective-permute-done.3 = bf16[512,256]{1,0:T(8,128)(2,1)S(1)} collective-permute-done((bf16[512,256]{1,0:T(8,128)(2,1)S(1)}, bf16[512,256]{1,0:T(8,128)(2,1)S(1)}, u32[]{:S(2)}, u32[]{:S(2)}) %collective-permute-start.3) | collective-permute-done | bytes 262176 | tf_op jit(solution)/shard_map/ppermute | solution.py:275
  80.8 0.1 add_convert_fusion
  80.9 0.7 slice_bitcast_fusion
Async XLA Ops:
  2.6 12.7 %all-to-all-start.1 = ((bf16[16,32,256]{2,1,0:T(8,128)(2,1)}), bf16[16,32,256]{2,1,0:T(8,128)(2,1)S(1)}, u32[]{:S(2)}, u32[]{:S(2)}) async-start(bf16[16,32,256]{2,1,0:T(8,128)(2,1)} %shard_map.94), calls=%async_computation.1 | async-start | bytes 524288 | tf_op jit(solution)/shard_map/all_to_all | solution.py:279
  11.7 1.3 %copy-start = (bf16[16,32,2048]{2,1,0:T(8,128)(2,1)}, bf16[16,32,2048]{2,1,0:T(8,128)(2,1)S(1)}, u32[]{:S(2)}) copy-start(bf16[16,32,2048]{2,1,0:T(8,128)(2,1)S(1)} %shard_map.93) | copy-start | bytes 6291460
  15.3 35.9 %all-to-all-start = ((bf16[16,32,2048]{2,1,0:T(8,128)(2,1)}), bf16[16,32,2048]{2,1,0:T(8,128)(2,1)S(1)}, u32[]{:S(2)}, u32[]{:S(2)}) async-start(bf16[16,32,2048]{2,1,0:T(8,128)(2,1)} %copy-done), calls=%async_computation | async-start | bytes 4194304 | tf_op jit(solution)/shard_map/all_to_all | solution.py:279
  19.5 11.7 %collective-permute-start.1 = (bf16[512,256]{1,0:T(8,128)(2,1)S(1)}, bf16[512,256]{1,0:T(8,128)(2,1)S(1)}, u32[]{:S(2)}, u32[]{:S(2)}) collective-permute-start(bf16[512,256]{1,0:T(8,128)(2,1)S(1)} %bitcast.15), channel_id=1, source_target_pairs={{0,16},{8,24},{16,32},{24,40},{32,48},{40,56},{48,64},{56,72},{64,... | collective-permute-start | bytes 786440 | tf_op jit(solution)/shard_map/ppermute | solution.py:275
  24.6 26.7 %collective-permute-start = (bf16[512,256]{1,0:T(8,128)(2,1)S(1)}, bf16[512,256]{1,0:T(8,128)(2,1)S(1)}, u32[]{:S(2)}, u32[]{:S(2)}) collective-permute-start(bf16[512,256]{1,0:T(8,128)(2,1)S(1)} %bitcast.16), channel_id=1, source_target_pairs={{0,8},{8,16},{16,24},{24,32},{32,40},{40,48},{48,56},{56,64},{64,7... | collective-permute-start | bytes 786440 | tf_op jit(solution)/shard_map/ppermute | solution.py:275
  65.0 11.8 %collective-permute-start.2 = (bf16[512,256]{1,0:T(8,128)(2,1)S(1)}, bf16[512,256]{1,0:T(8,128)(2,1)S(1)}, u32[]{:S(2)}, u32[]{:S(2)}) collective-permute-start(bf16[512,256]{1,0:T(8,128)(2,1)S(1)} %get-tuple-element.20), channel_id=1, source_target_pairs={{16,0},{24,8},{32,16},{40,24},{48,32},{56,40},{64,48},{72,56},{80,... | collective-permute-start | bytes 786440 | tf_op jit(solution)/shard_map/ppermute | solution.py:275
  67.1 13.7 %collective-permute-start.3 = (bf16[512,256]{1,0:T(8,128)(2,1)S(1)}, bf16[512,256]{1,0:T(8,128)(2,1)S(1)}, u32[]{:S(2)}, u32[]{:S(2)}) collective-permute-start(bf16[512,256]{1,0:T(8,128)(2,1)S(1)} %get-tuple-element.21), channel_id=1, source_target_pairs={{8,0},{16,8},{24,16},{32,24},{40,32},{48,40},{56,48},{64,56},{72,6... | collective-permute-start | bytes 786440 | tf_op jit(solution)/shard_map/ppermute | solution.py:275

commit v4 on v3

--- a/solution.py
+++ b/solution.py
@@ -10,7 +10,6 @@
 
 HD = 128
 SPAN = 2
-FRONT_HEADS = 4
 BACK_HEADS = 4
 PACK_SLOTS = 2
 TILE = 256
@@ -136,34 +135,44 @@
     block_rows = rows_ref.shape[0]
     margin = SPAN * block_rows
     width = margin + TILE
-    for head in range(0, heads, FRONT_HEADS):
-        for t in range(block_rows // TILE):
-            here = slice(t * TILE, (t + 1) * TILE)
-            window = slice(t * TILE, t * TILE + width)
-            query = stacked(rows_ref, here, head * HD, FRONT_HEADS)
-            grad = stacked(rows_ref, here, (heads + head) * HD, FRONT_HEADS)
-            scores = dot(query, key_win[window, :], NT)
-            if head == 0:
-                bias_ref[here, :] = mask(begin_ref[here, :1] - t * TILE, margin, width)
-            scores = (scores * LOG2_SCALE).reshape(FRONT_HEADS, TILE, width)
-            scores = (scores + bias_ref[here, :][None]).reshape(FRONT_HEADS * TILE, width)
-            top = jnp.max(scores, axis=1, keepdims=True)
-            expo = jnp.exp2(scores - top)
-            inverse = 1.0 / jnp.sum(expo, axis=1, keepdims=True)
-            prob = expo.astype(jnp.bfloat16)
-            dprob = dot(grad, value_win[window, :], NT)
-            delta = jnp.sum(expo * dprob, axis=1, keepdims=True) * inverse
-            dscore = (expo * (dprob - delta)).astype(jnp.bfloat16)
-            query = (query.astype(jnp.float32) * inverse).astype(jnp.bfloat16)
-            grad = (grad.astype(jnp.float32) * inverse).astype(jnp.bfloat16)
-            for h in range(FRONT_HEADS):
-                part = slice(h * TILE, (h + 1) * TILE)
-                prob_ref[head + h, here, :] = prob[part]
-                dscore_ref[head + h, here, :] = dscore[part]
-            before = margin - t * TILE
-            past = slice(t * TILE, margin)
-            dv_ref[:, past] += dot(grad, prob[:, :before], TN)
-            dk_ref[:, past] += dot(query, dscore[:, :before], TN)
+    units = [(head, t) for head in range(heads) for t in range(block_rows // TILE)]
+
+    def spans(t):
+        return slice(t * TILE, (t + 1) * TILE), slice(t * TILE, t * TILE + width)
+
+    def columns(head):
+        return slice(head * HD, (head + 1) * HD)
+
+    def masked_scores(head, t):
+        here, window = spans(t)
+        scores = dot(rows_ref[here, columns(head)], key_win[window, :], NT)
+        if head == 0:
+            bias_ref[here, :] = mask(begin_ref[here, :1] - t * TILE, margin, width)
+        scores = scores * LOG2_SCALE + bias_ref[here, :]
+        return scores, jnp.max(scores, axis=1, keepdims=True)
+
+    coming = masked_scores(*units[0])
+    for index, (head, t) in enumerate(units):
+        here, window = spans(t)
+        scores, top = coming
+        query = rows_ref[here, columns(head)]
+        grad = rows_ref[here, columns(heads + head)]
+        dprob = dot(grad, value_win[window, :], NT)
+        if index + 1 < len(units):
+            coming = masked_scores(*units[index + 1])
+        expo = jnp.exp2(scores - top)
+        inverse = 1.0 / jnp.sum(expo, axis=1, keepdims=True)
+        prob = expo.astype(jnp.bfloat16)
+        delta = jnp.sum(expo * dprob, axis=1, keepdims=True) * inverse
+        dscore = (expo * (dprob - delta)).astype(jnp.bfloat16)
+        prob_ref[head, here, :] = prob
+        dscore_ref[head, here, :] = dscore
+        query = (query.astype(jnp.float32) * inverse).astype(jnp.bfloat16)
+        grad = (grad.astype(jnp.float32) * inverse).astype(jnp.bfloat16)
+        before = margin - t * TILE
+        past = slice(t * TILE, margin)
+        dv_ref[:, past] += dot(grad, prob[:, :before], TN)
+        dk_ref[:, past] += dot(query, dscore[:, :before], TN)
     for place, ref in ((0, back2_ref), (1, back1_ref)):
         here = slice(place * block_rows, (place + 1) * block_rows)
         ref[:, :HD] = (dk_ref[:, here] * SCALE).T.astype(ref.dtype)
@@ -294,10 +303,12 @@
     attended, query_grad, own, back1, back2 = attend(
         rows, key_value, previous[0], previous[1], begin, heads
     )
-    for offset, part in ((2, back2), (1, back1)):
-        own = own + shifted(part, "ctx", -offset).astype(jnp.float32)
-    own = own.astype(jnp.bfloat16)
-    return (attended[None], query_grad[None], own[None, :, :HD], own[None, :, HD:])
+    two, one = shifted(back2, "ctx", -2), shifted(back1, "ctx", -1)
+    key_grad, value_grad = (
+        (own[:, c] + two[:, c].astype(jnp.float32) + one[:, c].astype(jnp.float32)).astype(two.dtype)
+        for c in (slice(0, HD), slice(HD, 2 * HD))
+    )
+    return (attended[None], query_grad[None], key_grad[None], value_grad[None])
 
 
 def solution(mesh):

time: 82 us -> 81.5 us (level)
  no operation moved by 1% of the time
where the time goes in v4:
time: 81.5 us; the launch traced here: 81 us
  waiting for transfers between devices  28.3 us (35%)
  Pallas kernels  27 us (33%)
  starting transfers between devices  22.9 us (28%)
  local copies, waits for them, and re-layouts  1.32 us (2%)
    ppermute x4, waiting for transfers between devices, shifted(): return lax.ppermute(block, axis, route)  26 us
    pallas_call x1, Pallas kernels, attend(): pl.pallas_call(functools.partial(front_kernel, heads), in_specs=[whole(be...  13.2 us
    ppermute x4, starting transfers between devices, shifted(): return lax.ppermute(block, axis, route)  12.7 us
    all_to_all x2, starting transfers between devices, exchange(): lax.all_to_all(block, ('tp', 'dp'), split_axis=0, concat_axis=0, tiled=True)  10.2 us
    pallas_call x1, Pallas kernels, attend(): pl.pallas_call(functools.partial(back_kernel, heads), in_specs=specs + [v...  7.81 us
    pallas_call x1, Pallas kernels, pack_large(): pl.pallas_call(pack_large_kernel, grid=(slots // PACK_SLOTS,), in_specs=[...  3.13 us
    all_to_all x2, waiting for transfers between devices, exchange(): lax.all_to_all(block, ('tp', 'dp'), split_axis=0, concat_axis=0, tiled=True)  2.33 us
    pallas_call x1, Pallas kernels, pack_small(): pl.pallas_call(pack_small_kernel, in_specs=[whole(order.shape), whole(key...  1.95 us
  transfers between devices with their start and end apart: 6, of which 4 were waited for; matrix products, arithmetic and copies ran while one was open for 0% of the time, Pallas kernels for 15%

profile of v4, /device:TPU:102, one launch (start us, length us, event | category | flops | bytes accessed | tf_op | source)
XLA Modules:
  0.0 81.0 jit_solution(9450174683995724301)
XLA Ops:
  0.6 1.9 %shard_map.94 = bf16[16,32,256]{2,1,0:T(8,128)(2,1)} custom-call(s32[1,64]{1,0:T(1,128)} %bitcast.23, bf16[64,1024]{1,0:T(8,128)(2,1)} %bitcast.21, bf16[64,1024]{1,0:T(8,128)(2,1)} %bitcast.22), custom_call_target="tpu_custom_call" | custom-call | tf_op jit(solution)/shard_map/pallas_call | solution.py:67
  2.6 5.9 %all-to-all-start.1 = ((bf16[16,32,256]{2,1,0:T(8,128)(2,1)}), bf16[16,32,256]{2,1,0:T(8,128)(2,1)S(1)}, u32[]{:S(2)}, u32[]{:S(2)}) async-start(bf16[16,32,256]{2,1,0:T(8,128)(2,1)} %shard_map.94), calls=%async_computation.1 | async-start | bytes 524288 | tf_op jit(solution)/shard_map/all_to_all | solution.py:288
  8.5 3.1 %shard_map.93 = bf16[16,32,2048]{2,1,0:T(8,128)(2,1)S(1)} custom-call(s32[1,64]{1,0:T(1,128)} %bitcast.24, bf16[64,8192]{1,0:T(8,128)(2,1)} %bitcast.19, bf16[64,8192]{1,0:T(8,128)(2,1)} %bitcast.20), custom_call_target="tpu_custom_call" | custom-call | tf_op jit(solution)/shard_map/pallas_call | solution.py:81
  11.7 0.0 copy-start
  11.7 1.3 %copy-done = bf16[16,32,2048]{2,1,0:T(8,128)(2,1)} copy-done((bf16[16,32,2048]{2,1,0:T(8,128)(2,1)}, bf16[16,32,2048]{2,1,0:T(8,128)(2,1)S(1)}, u32[]{:S(2)}) %copy-start) | copy-done | bytes 2097176
  13.0 2.3 %all-to-all-done.1 = bf16[16,32,256]{2,1,0:T(8,128)(2,1)S(1)} async-done(((bf16[16,32,256]{2,1,0:T(8,128)(2,1)}), bf16[16,32,256]{2,1,0:T(8,128)(2,1)S(1)}, u32[]{:S(2)}, u32[]{:S(2)}) %all-to-all-start.1) | async-done | bytes 262176 | tf_op jit(solution)/shard_map/all_to_all | solution.py:288
  15.3 4.2 %all-to-all-start = ((bf16[16,32,2048]{2,1,0:T(8,128)(2,1)}), bf16[16,32,2048]{2,1,0:T(8,128)(2,1)S(1)}, u32[]{:S(2)}, u32[]{:S(2)}) async-start(bf16[16,32,2048]{2,1,0:T(8,128)(2,1)} %copy-done), calls=%async_computation | async-start | bytes 4194304 | tf_op jit(solution)/shard_map/all_to_all | solution.py:288
  19.5 5.0 %collective-permute-start.1 = (bf16[512,256]{1,0:T(8,128)(2,1)S(1)}, bf16[512,256]{1,0:T(8,128)(2,1)S(1)}, u32[]{:S(2)}, u32[]{:S(2)}) collective-permute-start(bf16[512,256]{1,0:T(8,128)(2,1)S(1)} %bitcast.15), channel_id=1, source_target_pairs={{0,16},{8,24},{16,32},{24,40},{32,48},{40,56},{48,64},{56,72},{64,... | collective-permute-start | bytes 786440 | tf_op jit(solution)/shard_map/ppermute | solution.py:284
  24.6 3.8 %collective-permute-start = (bf16[512,256]{1,0:T(8,128)(2,1)S(1)}, bf16[512,256]{1,0:T(8,128)(2,1)S(1)}, u32[]{:S(2)}, u32[]{:S(2)}) collective-permute-start(bf16[512,256]{1,0:T(8,128)(2,1)S(1)} %bitcast.16), channel_id=1, source_target_pairs={{0,8},{8,16},{16,24},{24,32},{32,40},{40,48},{48,56},{56,64},{64,7... | collective-permute-start | bytes 786440 | tf_op jit(solution)/shard_map/ppermute | solution.py:284
  28.3 0.9 %shard_map.95.begin_ref = s32[512,128]{1,0:T(8,128)S(1)} custom-call(s32[1,32]{1,0:T(1,128)} %lengths_ref), custom_call_target="tpu_custom_call" | custom-call | tf_op jit(solution)/shard_map/pallas_call | solution.py:272
  29.3 2.0 %collective-permute-done.1.kv2_ref = bf16[512,256]{1,0:T(8,128)(2,1)S(1)} collective-permute-done((bf16[512,256]{1,0:T(8,128)(2,1)S(1)}, bf16[512,256]{1,0:T(8,128)(2,1)S(1)}, u32[]{:S(2)}, u32[]{:S(2)}) %collective-permute-start.1) | collective-permute-done | bytes 262176 | tf_op jit(solution)/shard_map/ppermute | solution.py:284
  31.2 20.0 %collective-permute-done.kv1_ref = bf16[512,256]{1,0:T(8,128)(2,1)S(1)} collective-permute-done((bf16[512,256]{1,0:T(8,128)(2,1)S(1)}, bf16[512,256]{1,0:T(8,128)(2,1)S(1)}, u32[]{:S(2)}, u32[]{:S(2)}) %collective-permute-start) | collective-permute-done | bytes 262176 | tf_op jit(solution)/shard_map/ppermute | solution.py:284
  51.3 0.0 all-to-all-done
  51.3 13.2 %shard_map.96 = (bf16[8,512,1280]{2,1,0:T(8,128)(2,1)S(1)}, bf16[8,512,1280]{2,1,0:T(8,128)(2,1)S(1)}, bf16[512,256]{1,0:T(8,128)(2,1)S(1)}, bf16[512,256]{1,0:T(8,128)(2,1)S(1)}) custom-call(s32[512,128]{1,0:T(8,128)S(1)} %shard_map.95.begin_ref, bf16[512,2048]{1,0:T(8,128)(2,1)S(1)} %bitcast.13, bf16[512,256]{1,0:T(8,128)(2,1)S(1)} %bitcast.17, ...), custom_call_target="tpu_custom_call" | custom-call | flops 4697620480 | bytes 41943040 | tf_op jit(solution)/shard_map/pallas_call | solution.py:245
  64.5 2.0 %collective-permute-start.2 = (bf16[512,256]{1,0:T(8,128)(2,1)S(1)}, bf16[512,256]{1,0:T(8,128)(2,1)S(1)}, u32[]{:S(2)}, u32[]{:S(2)}) collective-permute-start(bf16[512,256]{1,0:T(8,128)(2,1)S(1)} %get-tuple-element.20), channel_id=1, source_target_pairs={{16,0},{24,8},{32,16},{40,24},{48,32},{56,40},{64,48},{72,56},{80,... | collective-permute-start | bytes 786440 | tf_op jit(solution)/shard_map/ppermute | solution.py:284
  66.5 1.9 %collective-permute-start.3 = (bf16[512,256]{1,0:T(8,128)(2,1)S(1)}, bf16[512,256]{1,0:T(8,128)(2,1)S(1)}, u32[]{:S(2)}, u32[]{:S(2)}) collective-permute-start(bf16[512,256]{1,0:T(8,128)(2,1)S(1)} %get-tuple-element.21), channel_id=1, source_target_pairs={{8,0},{16,8},{24,16},{32,24},{40,32},{48,40},{56,48},{64,56},{72,6... | collective-permute-start | bytes 786440 | tf_op jit(solution)/shard_map/ppermute | solution.py:284
  68.4 7.8 %shard_map.97 = (bf16[512,1024]{1,0:T(8,128)(2,1)}, bf16[512,1024]{1,0:T(8,128)(2,1)}, f32[512,256]{1,0:T(8,128)S(1)}) custom-call(bf16[512,2048]{1,0:T(8,128)(2,1)S(1)} %bitcast.14, bf16[512,256]{1,0:T(8,128)(2,1)S(1)} %bitcast.18, bf16[512,256]{1,0:T(8,128)(2,1)S(1)} %collective-permute-done.kv1_ref, bf16[512,256]{1,0:T(8,128)(2,1)S(1)} %collective-permute-done.1.kv2_ref, ...), custom_call_target="tpu_custom_call" | custom-call | flops 3355443200 | bytes 41943040 | tf_op jit(solution)/shard_map/pallas_call | solution.py:257
  76.3 0.0 collective-permute-done.2
  76.3 4.0 %collective-permute-done.3 = bf16[512,256]{1,0:T(8,128)(2,1)S(1)} collective-permute-done((bf16[512,256]{1,0:T(8,128)(2,1)S(1)}, bf16[512,256]{1,0:T(8,128)(2,1)S(1)}, u32[]{:S(2)}, u32[]{:S(2)}) %collective-permute-start.3) | collective-permute-done | bytes 262176 | tf_op jit(solution)/shard_map/ppermute | solution.py:284
  80.2 0.8 fusion.1
Async XLA Ops:
  2.6 12.7 %all-to-all-start.1 = ((bf16[16,32,256]{2,1,0:T(8,128)(2,1)}), bf16[16,32,256]{2,1,0:T(8,128)(2,1)S(1)}, u32[]{:S(2)}, u32[]{:S(2)}) async-start(bf16[16,32,256]{2,1,0:T(8,128)(2,1)} %shard_map.94), calls=%async_computation.1 | async-start | bytes 524288 | tf_op jit(solution)/shard_map/all_to_all | solution.py:288
  11.7 1.3 %copy-start = (bf16[16,32,2048]{2,1,0:T(8,128)(2,1)}, bf16[16,32,2048]{2,1,0:T(8,128)(2,1)S(1)}, u32[]{:S(2)}) copy-start(bf16[16,32,2048]{2,1,0:T(8,128)(2,1)S(1)} %shard_map.93) | copy-start | bytes 6291460
  15.3 35.9 %all-to-all-start = ((bf16[16,32,2048]{2,1,0:T(8,128)(2,1)}), bf16[16,32,2048]{2,1,0:T(8,128)(2,1)S(1)}, u32[]{:S(2)}, u32[]{:S(2)}) async-start(bf16[16,32,2048]{2,1,0:T(8,128)(2,1)} %copy-done), calls=%async_computation | async-start | bytes 4194304 | tf_op jit(solution)/shard_map/all_to_all | solution.py:288
  19.5 11.7 %collective-permute-start.1 = (bf16[512,256]{1,0:T(8,128)(2,1)S(1)}, bf16[512,256]{1,0:T(8,128)(2,1)S(1)}, u32[]{:S(2)}, u32[]{:S(2)}) collective-permute-start(bf16[512,256]{1,0:T(8,128)(2,1)S(1)} %bitcast.15), channel_id=1, source_target_pairs={{0,16},{8,24},{16,32},{24,40},{32,48},{40,56},{48,64},{56,72},{64,... | collective-permute-start | bytes 786440 | tf_op jit(solution)/shard_map/ppermute | solution.py:284
  24.6 26.7 %collective-permute-start = (bf16[512,256]{1,0:T(8,128)(2,1)S(1)}, bf16[512,256]{1,0:T(8,128)(2,1)S(1)}, u32[]{:S(2)}, u32[]{:S(2)}) collective-permute-start(bf16[512,256]{1,0:T(8,128)(2,1)S(1)} %bitcast.16), channel_id=1, source_target_pairs={{0,8},{8,16},{16,24},{24,32},{32,40},{40,48},{48,56},{56,64},{64,7... | collective-permute-start | bytes 786440 | tf_op jit(solution)/shard_map/ppermute | solution.py:284
  64.5 11.7 %collective-permute-start.2 = (bf16[512,256]{1,0:T(8,128)(2,1)S(1)}, bf16[512,256]{1,0:T(8,128)(2,1)S(1)}, u32[]{:S(2)}, u32[]{:S(2)}) collective-permute-start(bf16[512,256]{1,0:T(8,128)(2,1)S(1)} %get-tuple-element.20), channel_id=1, source_target_pairs={{16,0},{24,8},{32,16},{40,24},{48,32},{56,40},{64,48},{72,56},{80,... | collective-permute-start | bytes 786440 | tf_op jit(solution)/shard_map/ppermute | solution.py:284
  66.5 13.7 %collective-permute-start.3 = (bf16[512,256]{1,0:T(8,128)(2,1)S(1)}, bf16[512,256]{1,0:T(8,128)(2,1)S(1)}, u32[]{:S(2)}, u32[]{:S(2)}) collective-permute-start(bf16[512,256]{1,0:T(8,128)(2,1)S(1)} %get-tuple-element.21), channel_id=1, source_target_pairs={{8,0},{16,8},{24,16},{32,24},{40,32},{48,40},{56,48},{64,56},{72,6... | collective-permute-start | bytes 786440 | tf_op jit(solution)/shard_map/ppermute | solution.py:284

commit v5 on v4

--- a/solution.py
+++ b/solution.py
@@ -303,9 +303,9 @@
     attended, query_grad, own, back1, back2 = attend(
         rows, key_value, previous[0], previous[1], begin, heads
     )
-    two, one = shifted(back2, "ctx", -2), shifted(back1, "ctx", -1)
+    one, two = shifted(back1, "ctx", -1), shifted(back2, "ctx", -2)
     key_grad, value_grad = (
-        (own[:, c] + two[:, c].astype(jnp.float32) + one[:, c].astype(jnp.float32)).astype(two.dtype)
+        (own[:, c] + one[:, c].astype(jnp.float32) + two[:, c].astype(jnp.float32)).astype(one.dtype)
         for c in (slice(0, HD), slice(HD, 2 * HD))
     )
     return (attended[None], query_grad[None], key_grad[None], value_grad[None])

time: 81.5 us -> 84.4 us (1.036)
  the two profiles are of different devices: /device:TPU:102 before, /device:TPU:96 now
where the time goes in v5:
time: 84.4 us; the launch traced here: 84 us
  waiting for transfers between devices  27.2 us (32%)
  Pallas kernels  27 us (32%)
  starting transfers between devices  26.9 us (32%)
  local copies, waits for them, and re-layouts  1.32 us (2%)
    ppermute x4, waiting for transfers between devices, shifted(): return lax.ppermute(block, axis, route)  24.3 us
    ppermute x4, starting transfers between devices, shifted(): return lax.ppermute(block, axis, route)  17.6 us
    pallas_call x1, Pallas kernels, attend(): pl.pallas_call(functools.partial(front_kernel, heads), in_specs=[whole(be...  13.2 us
    all_to_all x2, starting transfers between devices, exchange(): lax.all_to_all(block, ('tp', 'dp'), split_axis=0, concat_axis=0, tiled=True)  9.22 us
    pallas_call x1, Pallas kernels, attend(): pl.pallas_call(functools.partial(back_kernel, heads), in_specs=specs + [v...  7.82 us
    pallas_call x1, Pallas kernels, pack_large(): pl.pallas_call(pack_large_kernel, grid=(slots // PACK_SLOTS,), in_specs=[...  3.14 us
    all_to_all x2, waiting for transfers between devices, exchange(): lax.all_to_all(block, ('tp', 'dp'), split_axis=0, concat_axis=0, tiled=True)  2.94 us
    pallas_call x1, Pallas kernels, pack_small(): pl.pallas_call(pack_small_kernel, in_specs=[whole(order.shape), whole(key...  1.95 us
  transfers between devices with their start and end apart: 6, of which 4 were waited for; matrix products, arithmetic and copies ran while one was open for 0% of the time, Pallas kernels for 14%

profile of v5, /device:TPU:96, one launch (start us, length us, event | category | flops | bytes accessed | tf_op | source)
XLA Modules:
  0.0 84.0 jit_solution(8333666883004879342)
XLA Ops:
  0.6 1.9 %shard_map.94 = bf16[16,32,256]{2,1,0:T(8,128)(2,1)} custom-call(s32[1,64]{1,0:T(1,128)} %bitcast.23, bf16[64,1024]{1,0:T(8,128)(2,1)} %bitcast.21, bf16[64,1024]{1,0:T(8,128)(2,1)} %bitcast.22), custom_call_target="tpu_custom_call" | custom-call | tf_op jit(solution)/shard_map/pallas_call | solution.py:67
  2.6 5.5 %all-to-all-start.1 = ((bf16[16,32,256]{2,1,0:T(8,128)(2,1)}), bf16[16,32,256]{2,1,0:T(8,128)(2,1)S(1)}, u32[]{:S(2)}, u32[]{:S(2)}) async-start(bf16[16,32,256]{2,1,0:T(8,128)(2,1)} %shard_map.94), calls=%async_computation.1 | async-start | bytes 524288 | tf_op jit(solution)/shard_map/all_to_all | solution.py:288
  8.1 3.1 %shard_map.93 = bf16[16,32,2048]{2,1,0:T(8,128)(2,1)S(1)} custom-call(s32[1,64]{1,0:T(1,128)} %bitcast.24, bf16[64,8192]{1,0:T(8,128)(2,1)} %bitcast.19, bf16[64,8192]{1,0:T(8,128)(2,1)} %bitcast.20), custom_call_target="tpu_custom_call" | custom-call | tf_op jit(solution)/shard_map/pallas_call | solution.py:81
  11.2 0.0 copy-start
  11.2 1.3 %copy-done = bf16[16,32,2048]{2,1,0:T(8,128)(2,1)} copy-done((bf16[16,32,2048]{2,1,0:T(8,128)(2,1)}, bf16[16,32,2048]{2,1,0:T(8,128)(2,1)S(1)}, u32[]{:S(2)}) %copy-start) | copy-done | bytes 2097176
  12.6 2.9 %all-to-all-done.1 = bf16[16,32,256]{2,1,0:T(8,128)(2,1)S(1)} async-done(((bf16[16,32,256]{2,1,0:T(8,128)(2,1)}), bf16[16,32,256]{2,1,0:T(8,128)(2,1)S(1)}, u32[]{:S(2)}, u32[]{:S(2)}) %all-to-all-start.1) | async-done | bytes 262176 | tf_op jit(solution)/shard_map/all_to_all | solution.py:288
  15.5 3.7 %all-to-all-start = ((bf16[16,32,2048]{2,1,0:T(8,128)(2,1)}), bf16[16,32,2048]{2,1,0:T(8,128)(2,1)S(1)}, u32[]{:S(2)}, u32[]{:S(2)}) async-start(bf16[16,32,2048]{2,1,0:T(8,128)(2,1)} %copy-done), calls=%async_computation | async-start | bytes 4194304 | tf_op jit(solution)/shard_map/all_to_all | solution.py:288
  19.2 5.0 %collective-permute-start.1 = (bf16[512,256]{1,0:T(8,128)(2,1)S(1)}, bf16[512,256]{1,0:T(8,128)(2,1)S(1)}, u32[]{:S(2)}, u32[]{:S(2)}) collective-permute-start(bf16[512,256]{1,0:T(8,128)(2,1)S(1)} %bitcast.15), channel_id=1, source_target_pairs={{0,16},{8,24},{16,32},{24,40},{32,48},{40,56},{48,64},{56,72},{64,... | collective-permute-start | bytes 786440 | tf_op jit(solution)/shard_map/ppermute | solution.py:284
  24.3 4.6 %collective-permute-start = (bf16[512,256]{1,0:T(8,128)(2,1)S(1)}, bf16[512,256]{1,0:T(8,128)(2,1)S(1)}, u32[]{:S(2)}, u32[]{:S(2)}) collective-permute-start(bf16[512,256]{1,0:T(8,128)(2,1)S(1)} %bitcast.16), channel_id=1, source_target_pairs={{0,8},{8,16},{16,24},{24,32},{32,40},{40,48},{48,56},{56,64},{64,7... | collective-permute-start | bytes 786440 | tf_op jit(solution)/shard_map/ppermute | solution.py:284
  28.9 0.9 %shard_map.95.begin_ref = s32[512,128]{1,0:T(8,128)S(1)} custom-call(s32[1,32]{1,0:T(1,128)} %lengths_ref), custom_call_target="tpu_custom_call" | custom-call | tf_op jit(solution)/shard_map/pallas_call | solution.py:272
  29.8 0.4 collective-permute-done.1.kv2_ref
  30.3 19.2 %collective-permute-done.kv1_ref = bf16[512,256]{1,0:T(8,128)(2,1)S(1)} collective-permute-done((bf16[512,256]{1,0:T(8,128)(2,1)S(1)}, bf16[512,256]{1,0:T(8,128)(2,1)S(1)}, u32[]{:S(2)}, u32[]{:S(2)}) %collective-permute-start) | collective-permute-done | bytes 262176 | tf_op jit(solution)/shard_map/ppermute | solution.py:284
  49.4 0.0 all-to-all-done
  49.4 13.2 %shard_map.96 = (bf16[8,512,1280]{2,1,0:T(8,128)(2,1)S(1)}, bf16[8,512,1280]{2,1,0:T(8,128)(2,1)S(1)}, bf16[512,256]{1,0:T(8,128)(2,1)S(1)}, bf16[512,256]{1,0:T(8,128)(2,1)S(1)}) custom-call(s32[512,128]{1,0:T(8,128)S(1)} %shard_map.95.begin_ref, bf16[512,2048]{1,0:T(8,128)(2,1)S(1)} %bitcast.13, bf16[512,256]{1,0:T(8,128)(2,1)S(1)} %bitcast.17, ...), custom_call_target="tpu_custom_call" | custom-call | flops 4697620480 | bytes 41943040 | tf_op jit(solution)/shard_map/pallas_call | solution.py:245
  62.7 5.9 %collective-permute-start.2 = (bf16[512,256]{1,0:T(8,128)(2,1)S(1)}, bf16[512,256]{1,0:T(8,128)(2,1)S(1)}, u32[]{:S(2)}, u32[]{:S(2)}) collective-permute-start(bf16[512,256]{1,0:T(8,128)(2,1)S(1)} %get-tuple-element.20), channel_id=1, source_target_pairs={{8,0},{16,8},{24,16},{32,24},{40,32},{48,40},{56,48},{64,56},{72,6... | collective-permute-start | bytes 786440 | tf_op jit(solution)/shard_map/ppermute | solution.py:284
  68.6 2.0 %collective-permute-start.3 = (bf16[512,256]{1,0:T(8,128)(2,1)S(1)}, bf16[512,256]{1,0:T(8,128)(2,1)S(1)}, u32[]{:S(2)}, u32[]{:S(2)}) collective-permute-start(bf16[512,256]{1,0:T(8,128)(2,1)S(1)} %get-tuple-element.21), channel_id=1, source_target_pairs={{16,0},{24,8},{32,16},{40,24},{48,32},{56,40},{64,48},{72,56},{80,... | collective-permute-start | bytes 786440 | tf_op jit(solution)/shard_map/ppermute | solution.py:284
  70.7 7.8 %shard_map.97 = (bf16[512,1024]{1,0:T(8,128)(2,1)}, bf16[512,1024]{1,0:T(8,128)(2,1)}, f32[512,256]{1,0:T(8,128)S(1)}) custom-call(bf16[512,2048]{1,0:T(8,128)(2,1)S(1)} %bitcast.14, bf16[512,256]{1,0:T(8,128)(2,1)S(1)} %bitcast.18, bf16[512,256]{1,0:T(8,128)(2,1)S(1)} %collective-permute-done.kv1_ref, bf16[512,256]{1,0:T(8,128)(2,1)S(1)} %collective-permute-done.1.kv2_ref, ...), custom_call_target="tpu_custom_call" | custom-call | flops 3355443200 | bytes 41943040 | tf_op jit(solution)/shard_map/pallas_call | solution.py:257
  78.5 0.0 collective-permute-done.2
  78.5 4.7 %collective-permute-done.3 = bf16[512,256]{1,0:T(8,128)(2,1)S(1)} collective-permute-done((bf16[512,256]{1,0:T(8,128)(2,1)S(1)}, bf16[512,256]{1,0:T(8,128)(2,1)S(1)}, u32[]{:S(2)}, u32[]{:S(2)}) %collective-permute-start.3) | collective-permute-done | bytes 262176 | tf_op jit(solution)/shard_map/ppermute | solution.py:284
  83.2 0.8 fusion.1
Async XLA Ops:
  2.6 12.9 %all-to-all-start.1 = ((bf16[16,32,256]{2,1,0:T(8,128)(2,1)}), bf16[16,32,256]{2,1,0:T(8,128)(2,1)S(1)}, u32[]{:S(2)}, u32[]{:S(2)}) async-start(bf16[16,32,256]{2,1,0:T(8,128)(2,1)} %shard_map.94), calls=%async_computation.1 | async-start | bytes 524288 | tf_op jit(solution)/shard_map/all_to_all | solution.py:288
  11.2 1.3 %copy-start = (bf16[16,32,2048]{2,1,0:T(8,128)(2,1)}, bf16[16,32,2048]{2,1,0:T(8,128)(2,1)S(1)}, u32[]{:S(2)}) copy-start(bf16[16,32,2048]{2,1,0:T(8,128)(2,1)S(1)} %shard_map.93) | copy-start | bytes 6291460
  15.5 33.9 %all-to-all-start = ((bf16[16,32,2048]{2,1,0:T(8,128)(2,1)}), bf16[16,32,2048]{2,1,0:T(8,128)(2,1)S(1)}, u32[]{:S(2)}, u32[]{:S(2)}) async-start(bf16[16,32,2048]{2,1,0:T(8,128)(2,1)} %copy-done), calls=%async_computation | async-start | bytes 4194304 | tf_op jit(solution)/shard_map/all_to_all | solution.py:288
  19.2 11.0 %collective-permute-start.1 = (bf16[512,256]{1,0:T(8,128)(2,1)S(1)}, bf16[512,256]{1,0:T(8,128)(2,1)S(1)}, u32[]{:S(2)}, u32[]{:S(2)}) collective-permute-start(bf16[512,256]{1,0:T(8,128)(2,1)S(1)} %bitcast.15), channel_id=1, source_target_pairs={{0,16},{8,24},{16,32},{24,40},{32,48},{40,56},{48,64},{56,72},{64,... | collective-permute-start | bytes 786440 | tf_op jit(solution)/shard_map/ppermute | solution.py:284
  24.3 25.2 %collective-permute-start = (bf16[512,256]{1,0:T(8,128)(2,1)S(1)}, bf16[512,256]{1,0:T(8,128)(2,1)S(1)}, u32[]{:S(2)}, u32[]{:S(2)}) collective-permute-start(bf16[512,256]{1,0:T(8,128)(2,1)S(1)} %bitcast.16), channel_id=1, source_target_pairs={{0,8},{8,16},{16,24},{24,32},{32,40},{40,48},{48,56},{56,64},{64,7... | collective-permute-start | bytes 786440 | tf_op jit(solution)/shard_map/ppermute | solution.py:284
  62.7 15.8 %collective-permute-start.2 = (bf16[512,256]{1,0:T(8,128)(2,1)S(1)}, bf16[512,256]{1,0:T(8,128)(2,1)S(1)}, u32[]{:S(2)}, u32[]{:S(2)}) collective-permute-start(bf16[512,256]{1,0:T(8,128)(2,1)S(1)} %get-tuple-element.20), channel_id=1, source_target_pairs={{8,0},{16,8},{24,16},{32,24},{40,32},{48,40},{56,48},{64,56},{72,6... | collective-permute-start | bytes 786440 | tf_op jit(solution)/shard_map/ppermute | solution.py:284
  68.6 14.5 %collective-permute-start.3 = (bf16[512,256]{1,0:T(8,128)(2,1)S(1)}, bf16[512,256]{1,0:T(8,128)(2,1)S(1)}, u32[]{:S(2)}, u32[]{:S(2)}) collective-permute-start(bf16[512,256]{1,0:T(8,128)(2,1)S(1)} %get-tuple-element.21), channel_id=1, source_target_pairs={{16,0},{24,8},{32,16},{40,24},{48,32},{56,40},{64,48},{72,56},{80,... | collective-permute-start | bytes 786440 | tf_op jit(solution)/shard_map/ppermute | solution.py:284
